TPU v7x, 32 devices: a whole 2x2x4 slice. The times are simulated.
32 devices in a mesh: line: 4 (over y, x), stream: 4 (over z), span: 2 (over core).
Axes of the slice: x: 2, y: 2, z: 4, core: 2. Of those that a mesh axis runs over, the one named last changes fastest.
Arguments:
- velocity: float32 [3, 256, 16, 512], P(None, 'line', 'span', 'stream'), may hold values from -6 to 6
- cotangent: float32 [3, 256, 16, 512], P(None, 'line', 'span', 'stream'), may hold values from -6 to 6
- in_weight: bfloat16 [2048, 128], replicated, may hold values from -0.5 to 0.5
- in_bias: float32 [2048], replicated, may hold values from -3 to 3
- out_weight: bfloat16 [3, 2048], replicated, may hold values from -0.125 to 0.125
- diffusion: float32 [256], replicated, may hold values from 1000 to 10000
- stencil: int32 [2, 128], replicated, may hold values from 0 to 23
- wall_mask: int32 [2, 16, 512], P(None, 'span', 'stream'), may hold values 0 or 1
Outputs:
- new_velocity: float32 [3, 256, 16, 512], P(None, 'line', 'span', 'stream')
- adjoint_velocity: float32 [3, 256, 16, 512], P(None, 'line', 'span', 'stream')
- grad_in_weight: float32 [2048, 128], P('line')
- grad_in_bias: float32 [2048], P('line')
- grad_out_weight: float32 [3, 2048], P(None, 'line')
Inputs may be any that keep to these rules, and one draw needn't show every extreme that they name: stencil[w, f] reads component stencil[w, f] // 8 at stencil[w, f] % 8 rows from wall w.
All inputs are finite; a program needn't handle non-finite values. No bound on the sum of `wall_mask` on one device may be relied on, other than what follows from the above.
Results may differ from a plain program's by a relative error of at most 0.012.
Values sent between devices are 32-bit elements; how exact they have to be, the bound alone decides.
A program may use at most 64 MiB of HBM per device.

v0:
```python
import jax
import jax.numpy as jnp
from jax import lax
from jax.sharding import PartitionSpec as P

WALL_ROWS = 8


ADVECT = 0.2


def prefix_2(part, axis, combine, identity, reverse):
    count = lax.axis_size(axis)
    place = lax.axis_index(axis)
    ahead = count - 1 - place if reverse else place
    gathered = jax.tree.map(lambda a: lax.all_gather(a, axis), part)
    state = jax.tree.map(lambda a, e: jnp.zeros_like(a) + jnp.asarray(e, a.dtype), part, identity)

    def one(hop, state):
        source = count - 1 - hop if reverse else hop
        return combine(
            state, jax.tree.map(lambda a: lax.dynamic_index_in_dim(a, source, 0, False), gathered)
        )

    return lax.fori_loop(0, ahead, one, state)


def padded_2(shard, sides, width):
    for axis, dim in sides:
        peers, length = (lax.axis_size(axis), shard.shape[dim])
        up = [(i, (i + 1) % peers) for i in range(peers)]
        down = [(j, i) for i, j in up]
        last = lax.slice_in_dim(shard, length - width, length, axis=dim)
        leading = lax.slice_in_dim(shard, 0, width, axis=dim)
        before = lax.ppermute(last, axis, up)
        after = lax.ppermute(leading, axis, down)
        shard = jnp.concatenate([before, shard, after], axis=dim)
    return shard


def thomas(sub_coef, main_coef, sup_coef, rhs):

    def forward(carried, row_data):
        ratio_prev, reduced_prev = carried
        sub_val, main_val, sup_val, rhs_row = row_data
        divisor = main_val - sub_val * ratio_prev
        ratio_new = sup_val / divisor
        reduced_new = (rhs_row - sub_val * reduced_prev) / divisor
        return ((ratio_new, reduced_new), (ratio_new, reduced_new))

    start = (jnp.zeros((), jnp.float32), jnp.zeros(rhs.shape[1:], jnp.float32))
    _, (ratio_all, reduced_all) = lax.scan(forward, start, (sub_coef, main_coef, sup_coef, rhs))

    def backward(value_next, row_data):
        ratio_row, reduced_row = row_data
        value_row = reduced_row - ratio_row * value_next
        return (value_row, value_row)

    _, solved = lax.scan(
        backward, jnp.zeros(rhs.shape[1:], jnp.float32), (ratio_all, reduced_all), reverse=True
    )
    return solved


def segment_join(left_part, right_part):
    left_alpha, left_delta, left_coupling = left_part
    right_alpha, right_delta, right_coupling = right_part
    divisor = 1.0 - left_coupling[3] * right_coupling[0]
    link_base = (left_delta + left_coupling[3] * right_alpha) / divisor
    link_prev = left_coupling[2] / divisor
    link_next = left_coupling[3] * right_coupling[1] / divisor
    far_base = right_alpha + right_coupling[0] * link_base
    far_prev = right_coupling[0] * link_prev
    far_next = right_coupling[1] + right_coupling[0] * link_next
    alpha_new = left_alpha + left_coupling[1] * far_base
    delta_new = right_delta + right_coupling[2] * link_base
    coupling_new = jnp.stack(
        [
            left_coupling[0] + left_coupling[1] * far_prev,
            left_coupling[1] * far_next,
            right_coupling[2] * link_prev,
            right_coupling[3] + right_coupling[2] * link_next,
        ]
    )
    return (alpha_new, delta_new, coupling_new)


def segment_flip(earlier, later):
    return segment_join(later, earlier)


def line_solve(rhs, sub_coef, sup_coef, inverse):
    row_count = rhs.shape[1]
    local_part = jnp.einsum("ij,cjzx->cizx", inverse, rhs, precision=lax.Precision.HIGHEST)
    first_column = inverse[:, 0]
    last_column = inverse[:, row_count - 1]
    below_gain = -sub_coef[0]
    above_gain = -sup_coef[row_count - 1]
    coupling = jnp.stack(
        [
            below_gain * first_column[0],
            above_gain * last_column[0],
            below_gain * first_column[row_count - 1],
            above_gain * last_column[row_count - 1],
        ]
    )
    own_alpha = local_part[:, 0]
    own_delta = local_part[:, row_count - 1]
    own_segment = (own_alpha, own_delta, coupling)
    identity = (
        jnp.zeros_like(own_alpha),
        jnp.zeros_like(own_delta),
        jnp.array([0.0, 1.0, 1.0, 0.0], jnp.float32),
    )
    prefix = prefix_2(own_segment, "line", segment_join, identity, False)
    suffix = prefix_2(own_segment, "line", segment_flip, identity, True)
    prefix_alpha, prefix_delta, prefix_coupling = prefix
    suffix_alpha, suffix_delta, suffix_coupling = suffix
    mat_aa = 1.0 - prefix_coupling[3] * coupling[0]
    mat_ab = -prefix_coupling[3] * coupling[1]
    mat_ba = -suffix_coupling[0] * coupling[2]
    mat_bb = 1.0 - suffix_coupling[0] * coupling[3]
    rhs_first = prefix_delta + prefix_coupling[3] * own_alpha
    rhs_second = suffix_alpha + suffix_coupling[0] * own_delta
    determinant = mat_aa * mat_bb - mat_ab * mat_ba
    value_prev = (rhs_first * mat_bb - mat_ab * rhs_second) / determinant
    value_next = (mat_aa * rhs_second - mat_ba * rhs_first) / determinant
    return (
        local_part
        + first_column[None, :, None, None] * (below_gain * value_prev)[:, None]
        + last_column[None, :, None, None] * (above_gain * value_next)[:, None]
    )


def pack_grads(totals):
    return jnp.concatenate([totals[0], totals[1][:, None], jnp.transpose(totals[2])], axis=1)


def unpack_grads(packed_rows, feature_count):
    weight_in = packed_rows[:, :feature_count]
    bias_in = packed_rows[:, feature_count]
    weight_out = jnp.transpose(packed_rows[:, feature_count + 1 :])
    return (weight_in, bias_in, weight_out)


def local(velocity, cotangent, in_weight, in_bias, out_weight, diffusion, stencil, wall_mask):
    line_count = lax.axis_size("line")
    line_index = lax.axis_index("line")
    row_count = velocity.shape[1]
    plane_count = velocity.shape[2]
    cell_count = velocity.shape[3]
    above_all = jnp.concatenate([diffusion[1:], diffusion[-1:]])
    face_below = lax.dynamic_slice_in_dim(diffusion, line_index * row_count, row_count)
    face_above = lax.dynamic_slice_in_dim(above_all, line_index * row_count, row_count)
    sub_coef = -face_below
    sup_coef = -face_above
    main_coef = 1.0 + face_below + face_above
    inverse = thomas(sub_coef, main_coef, sup_coef, jnp.eye(row_count, dtype=jnp.float32))
    padded = padded_2(velocity, (("stream", 3), ("span", 2)), 1)
    grad_stream = padded[:, :, 1:-1, 2:] - padded[:, :, 1:-1, :-2]
    grad_span = padded[:, :, 2:, 1:-1] - padded[:, :, :-2, 1:-1]
    explicit = velocity - ADVECT * (velocity[0] * grad_stream + velocity[2] * grad_span)
    at_top = line_index == line_count - 1
    at_wall = jnp.logical_or(line_index == 0, at_top)
    slab_bottom = velocity[:, :WALL_ROWS]
    slab_top = velocity[:, row_count - WALL_ROWS :][:, ::-1]
    wall_slab = jnp.where(at_top, slab_top, slab_bottom).reshape(
        3 * WALL_ROWS, plane_count, cell_count
    )
    pick_rows = jnp.where(at_top, stencil[1], stencil[0])
    column_mask = jnp.where(at_top, wall_mask[1], wall_mask[0]) * at_wall.astype(jnp.int32)
    mask_float = column_mask.astype(jnp.float32)
    features = jnp.take(wall_slab, pick_rows, axis=0).astype(jnp.bfloat16)
    feature_planes = jnp.transpose(features, (1, 0, 2))

    def one_plane(plane_feats):
        hidden = jnp.tanh(
            jnp.dot(in_weight, plane_feats, preferred_element_type=jnp.float32) + in_bias[:, None]
        ).astype(jnp.bfloat16)
        return (hidden, jnp.dot(out_weight, hidden, preferred_element_type=jnp.float32))

    hidden_planes, stress_planes = lax.map(one_plane, feature_planes)
    wall_source = jnp.transpose(stress_planes, (1, 0, 2)) * mask_float[None]
    rhs = explicit.at[:, 0].add(jnp.where(at_top, 0.0, wall_source))
    rhs = rhs.at[:, row_count - 1].add(jnp.where(at_top, wall_source, 0.0))
    new_velocity = line_solve(rhs, sub_coef, sup_coef, inverse)
    multiplier = line_solve(cotangent, sub_coef, sup_coef, inverse)
    stress_grad = (
        jnp.where(at_top, multiplier[:, row_count - 1], multiplier[:, 0]) * mask_float[None]
    ).astype(jnp.bfloat16)
    grad_planes = jnp.transpose(stress_grad, (1, 0, 2))

    def closure_back(running, plane_data):
        plane_feats, hidden, plane_grad = plane_data
        grad_out = running[2] + lax.dot_general(
            plane_grad, hidden, (((1,), (1,)), ((), ())), preferred_element_type=jnp.float32
        )
        hidden_grad = lax.dot_general(
            out_weight, plane_grad, (((0,), (0,)), ((), ())), preferred_element_type=jnp.float32
        )
        hidden_float = hidden.astype(jnp.float32)
        pre_grad = (hidden_grad * (1.0 - hidden_float * hidden_float)).astype(jnp.bfloat16)
        grad_in = running[0] + lax.dot_general(
            pre_grad, plane_feats, (((1,), (1,)), ((), ())), preferred_element_type=jnp.float32
        )
        grad_bias = running[1] + jnp.sum(pre_grad.astype(jnp.float32), axis=1)
        feature_grad = lax.dot_general(
            in_weight, pre_grad, (((0,), (0,)), ((), ())), preferred_element_type=jnp.float32
        )
        return ((grad_in, grad_bias, grad_out), feature_grad)

    totals = (
        jnp.zeros(in_weight.shape, jnp.float32),
        jnp.zeros(in_bias.shape, jnp.float32),
        jnp.zeros(out_weight.shape, jnp.float32),
    )
    totals, feature_grads = lax.scan(
        closure_back, totals, (feature_planes, hidden_planes, grad_planes)
    )
    selector = (pick_rows[:, None] == jnp.arange(3 * WALL_ROWS)[None, :]).astype(jnp.float32)
    slab_grad = jnp.einsum(
        "fk,zfx->kzx", selector, feature_grads, precision=lax.Precision.HIGHEST
    ).reshape(3, WALL_ROWS, plane_count, cell_count)
    flux_stream = padded_2(velocity[0] * multiplier, (("stream", 3),), 1)
    flux_span = padded_2(velocity[2] * multiplier, (("span", 2),), 1)
    stream_diff = flux_stream[:, :, :, 2:] - flux_stream[:, :, :, :-2]
    span_diff = flux_span[:, :, 2:] - flux_span[:, :, :-2]
    adjoint = multiplier + ADVECT * (stream_diff + span_diff)
    adjoint = adjoint.at[0].add(-ADVECT * jnp.sum(multiplier * grad_stream, axis=0))
    adjoint = adjoint.at[2].add(-ADVECT * jnp.sum(multiplier * grad_span, axis=0))
    adjoint = adjoint.at[:, :WALL_ROWS].add(jnp.where(at_top, 0.0, slab_grad))
    adjoint = adjoint.at[:, row_count - WALL_ROWS :].add(jnp.where(at_top, slab_grad[:, ::-1], 0.0))
    feature_count = in_weight.shape[1]
    packed = pack_grads(totals)
    plane_total = lax.psum(packed, ("stream", "span"))
    summed = lax.psum_scatter(plane_total, "line", scatter_dimension=0, tiled=True)
    weight_in, bias_in, weight_out = unpack_grads(summed, feature_count)
    return (new_velocity, adjoint, weight_in, bias_in, weight_out)


def solution(mesh):
    placed = (
        P(None, "line", "span", "stream"),
        P(None, "line", "span", "stream"),
        P(),
        P(),
        P(),
        P(),
        P(),
        P(None, "span", "stream"),
    )
    return jax.shard_map(
        local,
        mesh=mesh,
        in_specs=placed,
        out_specs=(
            P(None, "line", "span", "stream"),
            P(None, "line", "span", "stream"),
            P("line", None),
            P("line"),
            P(None, "line"),
        ),
        check_vma=False,
    )
```

profile of v0, /device:TPU:0, one launch (start us, length us, event | category | flops | bytes accessed | tf_op | source)
XLA Modules:
  0.0 695.3 jit_solution(6300367853588350955)
XLA Ops:
  7.3 2.6 fusion.73
  9.9 2.0 copy.118
  11.9 3.0 collective-permute-start.1
  15.9 2.0 collective-permute-start
  21.4 292.3 %while.142 = (s32[]{:T(128)}, f32[]{:T(128)}, f32[64]{0:T(128)S(1)}, f32[64]{0:T(128)S(1)}, f32[64,64]{1,0:T(8,128)S(1)}, /*index=5*/f32[64]{0:T(128)S(1)}, f32[64]{0:T(128)S(1)}, f32[64]{0:T(128)S(1)}, f32[64,64]{1,0:T(8,128)S(1)}) while((s32[]{:T(128)}, f32[]{:T(128)}, f32[64]{0:T(128)S(1)}, f32[64]{0:T(128)S(1)}, ...), condition=%wide.region_3.4_spmd.clone.clone, body=%wide.region_2.3_spmd.clone.sunk.clone | while | flops 262 | bytes 1491 | solution.py:52
  313.7 91.5 %while.143 = (s32[]{:T(128)}, f32[64]{0:T(128)S(1)}, f32[64,64]{1,0:T(8,128)S(1)}, f32[64,64]{1,0:T(8,128)S(1)}, f32[64]{0:T(128)S(1)}) while((s32[]{:T(128)}, f32[64]{0:T(128)S(1)}, f32[64,64]{1,0:T(8,128)S(1)}, f32[64,64]{1,0:T(8,128)S(1)}, f32[64]{0:T(128)S(1)}) %tuple.306), condition=%wide.region_5.6_spmd.clone.clone, body=%wide.region_4.5_spmd.clone.sunk.clone | while | flops 196 | bytes 1395 | solution.py:59
  409.8 10.1 %all-reduce = f32[16]{0:T(128)S(1)} all-reduce(f32[16]{0:T(128)S(1)} %maximum_dynamic-update-slice_fusion), channel_id=3, replica_groups=mesh['line'=4,'stream'=4,'span'=2] {'line'}, use_global_device_ids=true, to_apply=%add | all-reduce | flops 16 | bytes 128
  421.0 7.3 %all-gather.4 = f32[12,1,8,128]{3,2,1,0:T(8,128)S(1)} all-gather(f32[3,1,8,128]{3,2,1,0:T(8,128)S(1)} %bitcast.528), channel_id=6, replica_groups=mesh['line'=4,'stream'=4,'span'=2] {'line'}, dimensions={0}, use_global_device_ids=true | all-gather | bytes 61440 | tf_op jit(solution)/shard_map/all_gather | solution.py:16
  428.3 8.2 %all-gather.3 = f32[12,1,8,128]{3,2,1,0:T(8,128)S(1)} all-gather(f32[3,1,8,128]{3,2,1,0:T(8,128)S(1)} %bitcast.515), channel_id=5, replica_groups=mesh['line'=4,'stream'=4,'span'=2] {'line'}, dimensions={0}, use_global_device_ids=true | all-gather | bytes 61440 | tf_op jit(solution)/shard_map/all_gather | solution.py:16
  438.3 35.9 %while.141 = (s32[]{:T(128)}, f32[3,8,128]{2,1,0:T(8,128)S(1)}, f32[4]{0:T(128)S(1)}, s32[]{:T(128)}, f32[4,3,8,128]{3,2,1,0:T(8,128)S(1)}, /*index=5*/f32[4,4]{1,0:T(4,128)S(1)}, f32[4,3,8,128]{3,2,1,0:T(8,128)S(1)}) while((s32[]{:T(128)}, f32[3,8,128]{2,1,0:T(8,128)S(1)}, f32[4]{0:T(128)S(1)}, s32[]{:T(128)}, ...), condition=%wide.region_13.14_spmd.clone, body=%wide.region_12.13_spmd.sunk.clone | while | flops 21536 | bytes 49603 | solution.py:25
  476.7 11.5 %while.137 = (s32[]{:T(128)}, bf16[8,2048,128]{1,2,0:T(8,128)(2,1)}, f32[8,3,128]{2,0,1:T(8,128)S(1)}, bf16[8,128,128]{2,1,0:T(8,128)(2,1)S(1)}, bf16[2048,128]{...) while((s32[]{:T(128)}, bf16[8,2048,128]{1,2,0:T(8,128)(2,1)}, ...), condition=%wide.region_1.2_spmd.clone, body=%wide.region_0.1_spmd.sunk.clone | while | flops 69206016 | bytes 2159193 | solution.py:182
  492.4 1.9 copy.72
  499.4 4.0 multiply_reduce_fusion
  503.5 2.2 broadcast_multiply_fusion.1
  510.6 2.9 convolution_bitcast_fusion.4
  513.5 32.7 %while.144 = (s32[]{:T(128)}, f32[2048,128]{1,0:T(8,128)S(1)}, f32[2048]{0:T(1024)S(1)}, f32[3,2048]{1,0:T(4,128)S(1)}, f32[8,128,128]{1,2,0:T(8,128)}, /*index=...) while((s32[]{:T(128)}, f32[2048,128]{1,0:T(8,128)S(1)}, ...), condition=%wide.region_18.19_spmd.clone.clone, body=%wide.region_16.18_spmd.clone.sunk.clone | while | flops 139737088 | bytes 5452416 | solution.py:217
  547.3 6.7 all-gather.2
  554.0 8.7 %all-gather = f32[12,1,8,128]{3,2,1,0:T(8,128)S(1)} all-gather(f32[3,1,8,128]{3,2,1,0:T(8,128)S(1)} %bitcast.517), channel_id=2, replica_groups=mesh['line'=4,'stream'=4,'span'=2] {'line'}, dimensions={0}, use_global_device_ids=true | all-gather | bytes 61440 | tf_op jit(solution)/shard_map/all_gather | solution.py:16
  562.7 36.5 %while.139 = (s32[]{:T(128)}, f32[3,8,128]{2,1,0:T(8,128)S(1)}, f32[4]{0:T(128)S(1)}, s32[]{:T(128)}, f32[4,3,8,128]{3,2,1,0:T(8,128)S(1)}, /*index=5*/f32[4,4]{1,0:T(4,128)S(1)}, f32[4,3,8,128]{3,2,1,0:T(8,128)S(1)}) while((s32[]{:T(128)}, f32[3,8,128]{2,1,0:T(8,128)S(1)}, f32[4]{0:T(128)S(1)}, s32[]{:T(128)}, ...), condition=%wide.region_9.10_spmd.clone, body=%wide.region_8.9_spmd.sunk.clone | while | flops 21536 | bytes 49603 | solution.py:25
  600.6 2.4 pad_maximum_fusion.4
  611.8 3.8 collective-permute-start.4
  621.7 2.7 fusion.43
  625.6 3.3 reduce-scatter.2.cloned.1.call-done
  630.4 53.6 %all-reduce.3.cloned.1.call-done = f32[512,132]{0,1:T(8,128)} async-done(((f32[512,132]{0,1:T(8,128)}), f32[512,132]{0,1:T(8,128)}) %all-reduce.3.cloned.1.call-update) | async-done | bytes 270352 | tf_op jit(solution)/shard_map/psum | solution.py:235
  (839 shorter events, 368.9 us)
Async XLA Ops:
  7.2 412.9 %copy-start = (f32[3,64,8,128]{3,2,1,0:T(8,128)S(1)}, f32[3,64,8,128]{3,2,1,0:T(8,128)}, u32[]{:S(2)}) copy-start(f32[3,64,8,128]{3,2,1,0:T(8,128)} %param.39) | copy-start | bytes 2359300
  7.2 401.1 %copy-start.26 = (u32[32]{0:T(128)S(1)}, u32[32]{0:T(128)}, u32[]{:S(2)}) copy-start(u32[32]{0:T(128)} %constant.393) | copy-start | bytes 388
  7.2 621.7 %reduce-scatter.2.cloned.1.call-start = ((), (), s32[]{:S(2)}) async-start(), calls=%async_computation.1 | async-start | bytes 1392640 | tf_op jit(solution)/shard_map/reduce_scatter | solution.py:236
  9.9 465.1 %copy-start.25 = (s32[2,128]{1,0:T(2,128)S(1)}, s32[2,128]{1,0:T(2,128)}, u32[]{:S(2)}) copy-start(s32[2,128]{1,0:T(2,128)} %param.44) | copy-start | bytes 3076
  11.9 482.3 %collective-permute-start.1 = (f32[3,64,8,1]{1,2,3,0:T(8,128)}, f32[3,64,8,1]{1,2,3,0:T(8,128)}, u32[]{:S(2)}, u32[]{:S(2)}) collective-permute-start(f32[3,64,8,1]{1,2,3,0:T(8,128)} %copy.118), channel_id=1, source_target_pairs={{0,2},{2,4},{4,6},{6,0},{1,3},{3,5},{5,7},{7,1},{8,10},{10,12},{12... | collective-permute-start | bytes 18440 | tf_op jit(solution)/shard_map/ppermute | solution.py:35
  15.9 476.5 %collective-permute-start = (f32[3,64,8,1]{1,2,3,0:T(8,128)}, f32[3,64,8,1]{1,2,3,0:T(8,128)}, u32[]{:S(2)}, u32[]{:S(2)}) collective-permute-start(f32[3,64,8,1]{1,2,3,0:T(8,128)} %copy.117), channel_id=1, source_target_pairs={{2,0},{4,2},{6,4},{0,6},{3,1},{5,3},{7,5},{1,7},{10,8},{12,10},{14... | collective-permute-start | bytes 18440 | tf_op jit(solution)/shard_map/ppermute | solution.py:36
  19.4 457.2 %copy-start.1 = (bf16[2048,128]{1,0:T(8,128)(2,1)S(1)}, bf16[2048,128]{1,0:T(8,128)(2,1)}, u32[]{:S(2)}) copy-start(bf16[2048,128]{1,0:T(8,128)(2,1)} %param.40) | copy-start | bytes 1572868
  19.4 457.2 %copy-start.14 = (bf16[3,2048]{1,0:T(4,128)(2,1)S(1)}, bf16[3,2048]{1,0:T(4,128)(2,1)}, u32[]{:S(2)}) copy-start(bf16[3,2048]{1,0:T(4,128)(2,1)} %param.42) | copy-start | bytes 36868
  19.4 457.2 %copy-start.15 = (f32[2048]{0:T(1024)S(1)}, f32[2048]{0:T(1024)}, u32[]{:S(2)}) copy-start(f32[2048]{0:T(1024)} %param.41) | copy-start | bytes 24580
  420.9 55.8 %copy-start.8 = (f32[3,64,8,128]{3,1,2,0:T(8,128)}, f32[3,64,8,128]{3,1,2,0:T(8,128)S(1)}, u32[]{:S(2)}) copy-start(f32[3,64,8,128]{3,1,2,0:T(8,128)S(1)} %convolution_bitcast_fusion.3) | copy-start | bytes 2359300
  476.7 11.5 %copy-start.17 = (s32[2,8,128]{2,1,0:T(8,128)S(1)}, s32[2,8,128]{2,1,0:T(8,128)}, u32[]{:S(2)}) copy-start(s32[2,8,128]{2,1,0:T(8,128)} %param.45) | copy-start | bytes 24580
  497.6 1.5 collective-permute-start.2
  497.7 1.7 collective-permute-start.3
  546.2 61.2 %copy-start.2 = (f32[3,64,8,128]{3,1,2,0:T(8,128)S(1)}, f32[3,64,8,128]{3,1,2,0:T(8,128)}, u32[]{:S(2)}) copy-start(f32[3,64,8,128]{3,1,2,0:T(8,128)} %get-tuple-element.994) | copy-start | bytes 2359300
  600.6 15.7 %copy-start.10 = (f32[3,64,8,128]{3,1,2,0:T(8,128)S(1)}, f32[3,64,8,128]{3,1,2,0:T(8,128)}, u32[]{:S(2)}) copy-start(f32[3,64,8,128]{3,1,2,0:T(8,128)} %convolution_bitcast_fusion.4) | copy-start | bytes 2359300
  600.6 15.7 %copy-start.19 = (f32[64]{0:T(128)S(1)}, f32[64]{0:T(128)}, u32[]{:S(2)}) copy-start(f32[64]{0:T(128)} %copy-done.18) | copy-start | bytes 772
  600.6 15.7 %copy-start.21 = (f32[64]{0:T(128)S(1)}, f32[64]{0:T(128)}, u32[]{:S(2)}) copy-start(f32[64]{0:T(128)} %copy-done.20) | copy-start | bytes 772
  603.0 13.5 %copy-start.24 = (s32[1,128]{1,0:T(1,128)S(1)}, s32[1,128]{1,0:T(1,128)}, u32[]{:S(2)}) copy-start(s32[1,128]{1,0:T(1,128)} %copy-done.23) | copy-start | bytes 1540
  603.1 80.9 %all-reduce.3.cloned.1.call-start = ((), (), s32[]{:S(2)}) async-start(), calls=%async_computation.2 | async-start | bytes 557056 | tf_op jit(solution)/shard_map/psum | solution.py:235
  606.9 14.8 %collective-permute-start.6 = (f32[3,64,1,128]{3,1,2,0:T(8,128)}, f32[3,64,1,128]{3,1,2,0:T(8,128)}, u32[]{:S(2)}, u32[]{:S(2)}) collective-permute-start(f32[3,64,1,128]{3,1,2,0:T(8,128)} %get-tuple-element.996), channel_id=1, source_target_pairs={{1,0},{0,1},{3,2},{2,3},{5,4},{4,5},{7,6},{6,7},{9,8},{8,9},{11,10... | collective-permute-start | bytes 294920 | tf_op jit(solution)/shard_map/ppermute | solution.py:36
  606.9 14.8 %collective-permute-start.7 = (f32[3,64,1,128]{3,1,2,0:T(8,128)}, f32[3,64,1,128]{3,1,2,0:T(8,128)}, u32[]{:S(2)}, u32[]{:S(2)}) collective-permute-start(f32[3,64,1,128]{3,1,2,0:T(8,128)} %get-tuple-element.997), channel_id=1, source_target_pairs={{0,1},{1,0},{2,3},{3,2},{4,5},{5,4},{6,7},{7,6},{8,9},{9,8},{10,11... | collective-permute-start | bytes 294920 | tf_op jit(solution)/shard_map/ppermute | solution.py:35
  608.8 12.9 %copy-start.7 = (f32[3,64,8,128]{3,1,2,0:T(8,128)S(1)}, f32[3,64,8,128]{3,1,2,0:T(8,128)}, u32[]{:S(2)}) copy-start(f32[3,64,8,128]{3,1,2,0:T(8,128)} %copy-done.6) | copy-start | bytes 2359300
  611.7 8.8 %collective-permute-start.5 = (f32[3,64,8,1]{1,2,3,0:T(8,128)S(1)}, f32[3,64,8,1]{1,2,3,0:T(8,128)S(1)}, u32[]{:S(2)}, u32[]{:S(2)}) collective-permute-start(f32[3,64,8,1]{1,2,3,0:T(8,128)S(1)} %copy.99), channel_id=1, source_target_pairs={{0,2},{2,4},{4,6},{6,0},{1,3},{3,5},{5,7},{7,1},{8,10},{10,12},{12... | collective-permute-start | bytes 18440 | tf_op jit(solution)/shard_map/ppermute | solution.py:35
  611.8 7.5 %collective-permute-start.4 = (f32[3,64,8,1]{1,2,3,0:T(8,128)S(1)}, f32[3,64,8,1]{1,2,3,0:T(8,128)S(1)}, u32[]{:S(2)}, u32[]{:S(2)}) collective-permute-start(f32[3,64,8,1]{1,2,3,0:T(8,128)S(1)} %copy.97), channel_id=1, source_target_pairs={{2,0},{4,2},{6,4},{0,6},{3,1},{5,3},{7,5},{1,7},{10,8},{12,10},{14... | collective-permute-start | bytes 18440 | tf_op jit(solution)/shard_map/ppermute | solution.py:36
  (14 other events, 93.5 us)
Sparse Core Ops, SparseCore 0:
  603.2 25.7 reduce-scatter.1
  631.3 52.6 all-reduce.2
where the time goes:
time: 701 us; the launch traced here: 695 us
  local copies, waits for them, and re-layouts  222 us (32%)
  loops' own time  178 us (25%)
  other arithmetic  116 us (17%)
  waiting for transfers between devices  58.1 us (8%)
  matrix products  48.5 us (7%)
  blocking collectives  41.1 us (6%)
  between operations  21.2 us (3%)
  starting transfers between devices  10.1 us (1%)
    dynamic_slice x256, local copies, waits for them, and re-layouts, thomas(): lax.scan(forward, start, (sub_coef, main_coef, sup_coef, rhs))  162 us
    another operation x1, loops' own time, thomas(): lax.scan(forward, start, (sub_coef, main_coef, sup_coef, rhs))  123 us
    psum x1, waiting for transfers between devices, local(): plane_total = lax.psum(packed, ('stream', 'span'))  53.6 us
    another operation x4, loops' own time, prefix_2(): return lax.fori_loop(0, ahead, one, state)  53.1 us
    sub x64, other arithmetic, backward(): value_row = reduced_row - ratio_row * value_next  45 us
    div x64, other arithmetic, forward(): reduced_new = (rhs_row - sub_val * reduced_prev) / divisor  41.4 us
    all_gather x4, blocking collectives, prefix_2(): gathered = jax.tree.map(lambda a: lax.all_gather(a, axis), part)  30.9 us
  transfers between devices with their start and end apart: 10, of which 4 were waited for; matrix products, arithmetic and copies ran while one was open for 45% of the time, Pallas kernels for 0%

commit v1 on v0

v1 whole, which is shorter than its diff:
```python
import jax
import jax.numpy as jnp
from jax import lax
from jax.experimental import pallas as pl
from jax.experimental.pallas import tpu as pltpu
from jax.sharding import PartitionSpec as P

WALL_ROWS = 8
ADVECT = 0.2
HIGHEST = lax.Precision.HIGHEST


def prefix_kernel(step_ref, start_ref, end_ref, out_ref, total_ref):
    step = step_ref[...]
    count = step.shape[1]
    lane = lax.broadcasted_iota(jnp.int32, step.shape, 1)
    head = lane == 0
    one = jnp.ones_like(step)
    zero = jnp.zeros_like(step)
    a, b = one, jnp.where(head, zero, step)
    c, d = jnp.where(head, zero, one), jnp.where(head, one, one + step)
    hop = 1
    while hop < count:
        keep = lane >= hop
        pa = jnp.where(keep, pltpu.roll(a, hop, 1), one)
        pb = jnp.where(keep, pltpu.roll(b, hop, 1), zero)
        pc = jnp.where(keep, pltpu.roll(c, hop, 1), zero)
        pd = jnp.where(keep, pltpu.roll(d, hop, 1), one)
        a, b, c, d = a * pa + b * pc, a * pb + b * pd, c * pa + d * pc, c * pb + d * pd
        hop *= 2
    flux = start_ref[...] + 1.0
    value = a + b * flux
    out_ref[...] = value
    total_ref[...] = c + d * flux + end_ref[...] * value


def green_factors(diffusion):
    count = diffusion.shape[0]
    faces = jnp.concatenate([diffusion, diffusion[-1:]])
    both = jnp.stack([faces[:-1], faces[:0:-1]])
    starts = jnp.broadcast_to(jnp.stack([faces[0], faces[-1]])[:, None], (2, count))
    ends = jnp.broadcast_to(jnp.stack([faces[-1], faces[0]])[:, None], (2, count))
    pad = ((0, 6), (0, 0))
    shape = jax.ShapeDtypeStruct((8, count), jnp.float32)
    values, totals = pl.pallas_call(prefix_kernel, out_shape=(shape, shape), name="green")(
        jnp.pad(1.0 / both, pad), jnp.pad(starts, pad), jnp.pad(ends, pad)
    )
    return values[0], values[1, ::-1], 1.0 / totals[0, count - 1]


def halos(shard, axis, dim):
    peers, length = lax.axis_size(axis), shard.shape[dim]
    last = lax.slice_in_dim(shard, length - 1, length, axis=dim)
    first = lax.slice_in_dim(shard, 0, 1, axis=dim)
    if peers == 2:
        both = lax.ppermute(jnp.concatenate([first, last], axis=dim), axis, [(0, 1), (1, 0)])
        return lax.slice_in_dim(both, 1, 2, axis=dim), lax.slice_in_dim(both, 0, 1, axis=dim)
    up = [(i, (i + 1) % peers) for i in range(peers)]
    return lax.ppermute(last, axis, up), lax.ppermute(first, axis, [(j, i) for i, j in up])


def difference(shard, sides, dim):
    before, after = sides
    length = shard.shape[dim]
    ahead = jnp.concatenate([lax.slice_in_dim(shard, 1, length, axis=dim), after], axis=dim)
    behind = jnp.concatenate([before, lax.slice_in_dim(shard, 0, length - 1, axis=dim)], axis=dim)
    return ahead - behind


def local(velocity, cotangent, in_weight, in_bias, out_weight, diffusion, stencil, wall_mask):
    line_count = lax.axis_size("line")
    line_index = lax.axis_index("line")
    _, row_count, planes, cells = velocity.shape
    columns = planes * cells
    hidden_count, feature_count = in_weight.shape
    share = hidden_count // line_count
    at_top = line_index == line_count - 1

    slab_bottom = velocity[:, :WALL_ROWS]
    slab_top = velocity[:, row_count - WALL_ROWS :][:, ::-1]
    own_slab = jnp.where(at_top, slab_top, slab_bottom).reshape(3 * WALL_ROWS, columns)
    slabs = lax.all_gather(own_slab, "line")
    walls = (slabs[0], slabs[line_count - 1])

    low, high, scale = green_factors(diffusion)
    all_rows = low.shape[0]
    low_own = lax.dynamic_slice_in_dim(low, line_index * row_count, row_count)
    high_own = lax.dynamic_slice_in_dim(high, line_index * row_count, row_count)
    rows = jnp.arange(row_count)
    green = (
        jnp.where(
            rows[:, None] >= rows[None, :],
            high_own[:, None] * low_own[None, :],
            low_own[:, None] * high_own[None, :],
        )
        * scale
    )
    operator = jnp.concatenate([green, low_own[None], high_own[None]])

    grad_stream = difference(velocity, halos(velocity, "stream", 3), 3)
    grad_span = difference(velocity, halos(velocity, "span", 2), 2)
    explicit = velocity - ADVECT * (velocity[0] * grad_stream + velocity[2] * grad_span)

    weight_in = lax.dynamic_slice_in_dim(in_weight, line_index * share, share, 0)
    bias_in = lax.dynamic_slice_in_dim(in_bias, line_index * share, share, 0)
    weight_out = lax.dynamic_slice_in_dim(out_weight, line_index * share, share, 1)
    slots = jnp.arange(3 * WALL_ROWS)
    pick = (stencil[:, :, None] == slots).astype(jnp.float32)
    features = jnp.concatenate(
        [
            jnp.dot(pick[w], walls[w], precision=HIGHEST)
            for w in range(2)
        ],
        axis=1,
    ).astype(jnp.bfloat16)
    hidden = jnp.tanh(
        jnp.dot(weight_in, features, preferred_element_type=jnp.float32) + bias_in[:, None]
    ).astype(jnp.bfloat16)
    stress_part = jnp.dot(weight_out, hidden, preferred_element_type=jnp.float32)

    both = jnp.concatenate([explicit, cotangent])
    solved = jnp.einsum("ij,cjzx->cizx", operator, both, precision=HIGHEST)
    sums = solved[:, row_count:].reshape(12, columns)
    stress_part = stress_part.reshape(3, 2, columns).reshape(6, columns)
    gathered = lax.all_gather(jnp.concatenate([sums, stress_part]), "line")
    part = gathered[:, :12].reshape(line_count, 6, 2, planes, cells)
    place = jnp.arange(line_count)
    below = (place < line_index).astype(jnp.float32)
    above = (place > line_index).astype(jnp.float32)
    sum_below = jnp.sum(part[:, :, 0] * below[:, None, None, None], axis=0) * scale
    sum_above = jnp.sum(part[:, :, 1] * above[:, None, None, None], axis=0) * scale
    mask_float = wall_mask.astype(jnp.float32)
    stress = jnp.sum(gathered[:, 12:], axis=0).reshape(3, 2, planes, cells) * mask_float[None]
    from_low = sum_below[:3] + stress[:, 0] * (low[0] * scale)
    from_high = sum_above[:3] + stress[:, 1] * (high[all_rows - 1] * scale)
    low_col, high_col = low_own[None, :, None, None], high_own[None, :, None, None]
    new_velocity = solved[:3, :row_count] + high_col * from_low[:, None] + low_col * from_high[:, None]
    multiplier = (
        solved[3:, :row_count] + high_col * sum_below[3:, None] + low_col * sum_above[3:, None]
    )

    wall_total = jnp.sum(part[:, 3:], axis=0)
    wall_multiplier = jnp.stack(
        [
            wall_total[:, 1] * (low[0] * scale),
            wall_total[:, 0] * (high[all_rows - 1] * scale),
        ],
        axis=1,
    )
    stress_grad = (wall_multiplier * mask_float[None]).astype(jnp.bfloat16).reshape(3, 2 * columns)
    hidden_grad = lax.dot_general(
        weight_out, stress_grad, (((0,), (0,)), ((), ())), preferred_element_type=jnp.float32
    )
    hidden_float = hidden.astype(jnp.float32)
    pre_grad = (hidden_grad * (1.0 - hidden_float * hidden_float)).astype(jnp.bfloat16)
    wide = jnp.concatenate([features, jnp.ones((1, 2 * columns), jnp.bfloat16)])
    grad_in = lax.dot_general(
        pre_grad, wide, (((1,), (1,)), ((), ())), preferred_element_type=jnp.float32
    )
    grad_out = lax.dot_general(
        hidden, stress_grad, (((1,), (1,)), ((), ())), preferred_element_type=jnp.float32
    )
    totals = lax.psum(jnp.concatenate([grad_in, grad_out], axis=1), ("stream", "span"))

    feature_grad = lax.dot_general(
        weight_in, pre_grad, (((0,), (0,)), ((), ())), preferred_element_type=jnp.float32
    )
    slab_part = jnp.stack(
        [
            lax.dot_general(
                pick[w],
                feature_grad[:, w * columns : (w + 1) * columns],
                (((0,), (0,)), ((), ())),
                precision=HIGHEST,
            )
            for w in range(2)
        ]
    )
    slab_sum = lax.psum(slab_part, "line")
    at_wall = jnp.logical_or(line_index == 0, at_top)
    slab_grad = jnp.where(at_top, slab_sum[1], slab_sum[0]) * at_wall.astype(jnp.float32)
    slab_grad = slab_grad.reshape(3, WALL_ROWS, planes, cells)

    flux_stream = velocity[0] * multiplier
    flux_span = velocity[2] * multiplier
    stream_diff = difference(flux_stream, halos(flux_stream, "stream", 3), 3)
    span_diff = difference(flux_span, halos(flux_span, "span", 2), 2)
    adjoint = multiplier + ADVECT * (stream_diff + span_diff)
    own = -ADVECT * jnp.stack(
        [
            jnp.sum(multiplier * grad_stream, axis=0),
            jnp.zeros(multiplier.shape[1:], jnp.float32),
            jnp.sum(multiplier * grad_span, axis=0),
        ]
    )
    edge = jnp.where(at_top, slab_grad[:, ::-1], slab_grad)
    rest = ((0, 0), (0, row_count - WALL_ROWS), (0, 0), (0, 0))
    rest_top = ((0, 0), (row_count - WALL_ROWS, 0), (0, 0), (0, 0))
    adjoint = adjoint + own + jnp.where(at_top, jnp.pad(edge, rest_top), jnp.pad(edge, rest))
    return (
        new_velocity,
        adjoint,
        totals[:, :feature_count],
        totals[:, feature_count],
        jnp.transpose(totals[:, feature_count + 1 :]),
    )


def solution(mesh):
    field = P(None, "line", "span", "stream")
    return jax.shard_map(
        local,
        mesh=mesh,
        in_specs=(field, field, P(), P(), P(), P(), P(), P(None, "span", "stream")),
        out_specs=(field, field, P("line", None), P("line"), P(None, "line")),
        check_vma=False,
    )
```

time: 701 us -> 211 us (0.30)
  loops' own time: 178 us -> 0 us
  local copies, waits for them, and re-layouts: 222 us -> 48.6 us
  other arithmetic: 116 us -> 20.4 us
  matrix products: 48.5 us -> 12.9 us
  waiting for transfers between devices: 58.1 us -> 83.1 us
  blocking collectives: 41.1 us -> 19.2 us
    another operation x8 -> x0, loops' own time: 178 us -> none  [the longest x1 123 us: thomas(): lax.scan(forward, start, (sub_coef, main_coef, sup_coef, rhs))]
    dynamic_slice x262 -> x5, local copies, waits for them, and re-layouts: 162 us -> 2.31 us  [the longest x2 0.78 us: local(): low_own = lax.dynamic_slice_in_dim(low, line_index * row_count, row_count)]
    sub x64 -> x1, other arithmetic: 45 us -> 3.45 us  [local(): velocity - ADVECT * (velocity[0] * grad_stream + velocity[2] * grad_span)]
    div x64 -> x1, other arithmetic: 41.4 us -> 0.01 us  [green_factors(): 1.0 / both]
    dot_general x51 -> x11, matrix products: 48.5 us -> 12.9 us  [the longest x1 2.23 us: local(): lax.dot_general(hidden, stress_grad, (((1,), (1,)), ((), ())), preferred_...]
    psum x1 -> x2, waiting for transfers between devices: 53.6 us -> 80.9 us  [the longest x1 41.1 us: local(): slab_sum = lax.psum(slab_part, 'line')]
    add x18 -> x1, other arithmetic: 15 us -> 2.73 us  [local(): adjoint + own]
    dynamic_update_slice x208 -> x0, local copies, waits for them, and re-layouts: 11.7 us -> none  [the longest x192 11.4 us: thomas(): lax.scan(forward, start, (sub_coef, main_coef, sup_coef, rhs))]
  transfers between devices with their start and end apart: 10 -> 8, of which waited for: 4 -> 3; matrix products, arithmetic and copies ran while one was open for 45% -> 22% of each run, Pallas kernels for 0% -> 1%
where the time goes in v1:
time: 211 us; the launch traced here: 210 us
  waiting for transfers between devices  83.1 us (39%)
  local copies, waits for them, and re-layouts  48.6 us (23%)
  other arithmetic  20.4 us (10%)
  blocking collectives  19.2 us (9%)
  between operations  16.6 us (8%)
  matrix products  12.9 us (6%)
  starting transfers between devices  7.37 us (3%)
    psum x1, waiting for transfers between devices, local(): slab_sum = lax.psum(slab_part, 'line')  41.1 us
    psum x1, waiting for transfers between devices, local(): lax.psum(jnp.concatenate([grad_in, grad_out], axis=1), ('stream', 'span'))  39.8 us
    unnamed x80, local copies, waits for them, and re-layouts  13.6 us
    all_gather x1, blocking collectives, local(): slabs = lax.all_gather(own_slab, 'line')  9.74 us
    all_gather x1, blocking collectives, local(): gathered = lax.all_gather(jnp.concatenate([sums, stress_part]), 'line')  9.5 us
  transfers between devices with their start and end apart: 8, of which 3 were waited for; matrix products, arithmetic and copies ran while one was open for 22% of the time, Pallas kernels for 1%

profile of v1, /device:TPU:0, one launch (start us, length us, event | category | flops | bytes accessed | tf_op | source)
XLA Modules:
  0.0 210.1 jit_solution(8965955776770127672)
XLA Ops:
  10.9 2.0 copy.89
  13.0 2.6 %collective-permute-start.1 = (f32[3,64,8,1]{1,2,3,0:T(8,128)}, f32[3,64,8,1]{1,2,3,0:T(8,128)}, u32[]{:S(2)}, u32[]{:S(2)}) collective-permute-start(f32[3,64,8,1]{1,2,3,0:T(8,128)} %copy.89), channel_id=1, source_target_pairs={{0,2},{2,4},{4,6},{6,0},{1,3},{3,5},{5,7},{7,1},{8,10},{10,12},{12... | collective-permute-start | bytes 18440 | tf_op jit(solution)/shard_map/ppermute | solution.py:59
  16.4 2.0 collective-permute-start
  23.2 1.9 green.1
  28.7 9.7 %all_gather.9 = f32[4,24,1024]{2,1,0:T(8,128)S(1)} all-gather(f32[1,24,1024]{2,1,0:T(8,128)S(1)} %fusion.22), channel_id=1, replica_groups=mesh['line'=4,'stream'=4,'span'=2] {'line'}, dimensions={0}, use_global_device_ids=true | all-gather | bytes 491520 | tf_op jit(solution)/shard_map/all_gather | solution.py:82
  45.3 1.8 pad_maximum_fusion
  47.1 1.7 tanh_convert_fusion
  55.0 2.2 %copy.69 = f32[3,64,8,128]{3,1,2,0:T(8,128)} copy(f32[3,64,8,128]{3,2,1,0:T(8,128)} %param.9) | data formatting | bytes 1572864 | tf_op args[1]
  58.5 1.9 copy.59
  60.4 1.9 copy.62
  63.4 3.4 %multiply_subtract_fusion = (f32[3,64,8,128]{3,1,2,0:T(8,128)S(1)}, f32[3,64,8,128]{3,1,2,0:T(8,128)}) fusion(f32[64,8,128]{2,0,1:T(8,128)S(1)} %copy.63, f32[64,8,128]{2,0,1:T(8,128)S(1)} %copy.56, f32[3,64,7,128]{3,1,2,0:T(8,128)S(1)} %copy-done.4, f32[3,64,1,128]{3,1,2,0:T(8,128)S(1)} %get-tuple-element.54, f32[3,64,1,128]{3,1,2,0:T(8,128)S(1)} %get-tuple-element.53, ...), kind=kLoop, calls=%fused_computation.27 | loop fusion | flops 2162688 | bytes 6029312 | tf_op jit(solution)/shard_map/sub | solution.py:102
  66.9 1.7 fusion.4
  68.7 9.5 %all-gather.1 = f32[4,18,1024]{2,1,0:T(8,128)S(1)} all-gather(f32[1,18,1024]{2,1,0:T(8,128)S(1)} %maximum_bitcast_fusion), channel_id=2, replica_groups=mesh['line'=4,'stream'=4,'span'=2] {'line'}, dimensions={0}, use_global_device_ids=true | all-gather | bytes 368640 | tf_op jit(solution)/shard_map/all_gather | solution.py:125
  79.5 1.7 reshape.76
  83.2 2.2 %fusion.44 = f32[512,3]{0,1:T(4,128)S(1)} fusion(bf16[512,2048]{1,0:T(8,128)(2,1)} %copy-done.2, f32[1,3,16,128]{3,2,1,0:T(8,128)S(1)} %maximum_bitcast_fusion.3, f32[2048]{0:T(1024)S(1)} %get-tuple-element.61), kind=kOutput, calls=%fused_computation.101 | convolution fusion | flops 6303744 | bytes 2136064 | tf_op jit(solution)/shard_map/dot_general | solution.py:160
  89.8 2.4 %multiply_reduce_fusion.1 = (f32[64,8,128]{2,0,1:T(8,128)}, f32[64,8,128]{2,0,1:T(8,128)}, f32[3,64,8,128]{3,1,2,0:T(8,128)S(1)}, f32[3,64,8,128]{3,1,2,0:T(8,128)S(1)}, f32[3,64,8,128]{3,1,2,0:T(8,128)}) fusion(f32[3,64,8,128]{3,1,2,0:T(8,128)S(1)} %copy-done.7, f32[3,8,128]{2,1,0:T(8,128)S(1)} %get-tuple-element.60, f32[64]{0:T(128)S(1)} %copy-done.28, ...), kind=kLoop, calls=%fused_computation.26 | loop fusion | flops 3211264 | bytes 7389696 | tf_op jit(solution)/shard_map/reduce_sum | solution.py:191
  100.4 1.8 collective-permute-start.3
  103.1 2.5 %copy.83 = f32[3,64,8,128]{3,2,1,0:T(8,128)} copy(f32[3,64,8,128]{3,1,2,0:T(8,128)} %get-tuple-element.30) | data formatting | bytes 1572864
  105.6 2.1 %collective-permute-done.4 = f32[3,64,8,1]{1,2,3,0:T(8,128)S(1)} collective-permute-done((f32[3,64,8,1]{1,2,3,0:T(8,128)S(1)}, f32[3,64,8,1]{1,2,3,0:T(8,128)S(1)}, u32[]{:S(2)}, u32[]{:S(2)}) %collective-permute-start.4) | collective-permute-done | bytes 6176 | tf_op jit(solution)/shard_map/ppermute | solution.py:59
  109.3 39.8 %all-reduce.11.cloned.1.call-done = f32[512,132]{0,1:T(8,128)} async-done(((f32[512,132]{0,1:T(8,128)}), f32[512,132]{0,1:T(8,128)}) %all-reduce.11.cloned.1.call-update) | async-done | bytes 270352 | tf_op jit(solution)/shard_map/psum | solution.py:163
  149.1 1.7 slice.292
  150.8 1.8 copy.85
  155.2 41.1 %all-reduce.9.cloned.1.call-done = f32[2,24,1024]{2,1,0:T(8,128)} async-done(((f32[2,24,1024]{2,1,0:T(8,128)}), f32[2,24,1024]{2,1,0:T(8,128)}) %all-reduce.9.cloned.1.call-update) | async-done | bytes 196624 | tf_op jit(solution)/shard_map/psum | solution.py:179
  199.2 2.7 %fusion.13 = f32[3,64,8,128]{3,1,2,0:T(8,128)S(1)} fusion(f32[3,64,8,1]{3,1,2,0:T(8,128)} %copy.79, f32[3,64,8,127]{3,1,2,0:T(8,128)} %get-tuple-element.38, f32[3,64,8,127]{3,1,2,0:T(8,128)} %get-tuple-element.37, f32[3,64,8,1]{3,1,2,0:T(8,128)S(1)} %copy.81, f32[3,64,1,128]{3,1,2,0:T(8,128)S(1)} %get-tuple-element.50, ...), kind=kLoop, calls=%fused_computation.22 | loop fusion | flops 3735552 | bytes 5366285 | tf_op jit(solution)/shard_map/add | solution.py:199
  (166 shorter events, 51.3 us)
Async XLA Ops:
  7.2 40.0 %copy-start = (bf16[2048,128]{1,0:T(8,128)(2,1)S(1)}, bf16[2048,128]{1,0:T(8,128)(2,1)}, u32[]{:S(2)}) copy-start(bf16[2048,128]{1,0:T(8,128)(2,1)} %param.10) | copy-start | bytes 1572868
  7.2 141.9 %all-reduce.11.cloned.1.call-start = ((), (), s32[]{:S(2)}) async-start(), calls=%async_computation.1 | async-start | bytes 557056 | tf_op jit(solution)/shard_map/psum | solution.py:163
  9.3 9.1 %copy-start.23 = (f32[256]{0:T(256)S(1)}, f32[256]{0:T(256)}, u32[]{:S(2)}) copy-start(f32[256]{0:T(256)} %param.13) | copy-start | bytes 3076
  9.3 53.0 %collective-permute-start.2 = (f32[3,64,2,128]{3,1,2,0:T(8,128)}, f32[3,64,2,128]{3,1,2,0:T(8,128)}, u32[]{:S(2)}, u32[]{:S(2)}) collective-permute-start(f32[3,64,2,128]{3,1,2,0:T(8,128)} %pad_maximum_fusion.2), channel_id=1, source_target_pairs={{0,1},{1,0},{2,3},{3,2},{4,5},{5,4},{6,7},{7,6},{8,9},{9,8},{10,11... | collective-permute-start | bytes 589832 | tf_op jit(solution)/shard_map/ppermute | solution.py:56
  10.9 17.6 %copy-start.30 = (s32[2,128]{1,0:T(2,128)S(1)}, s32[2,128]{1,0:T(2,128)}, u32[]{:S(2)}) copy-start(s32[2,128]{1,0:T(2,128)} %param.14) | copy-start | bytes 3076
  13.0 47.5 %collective-permute-start.1 = (f32[3,64,8,1]{1,2,3,0:T(8,128)}, f32[3,64,8,1]{1,2,3,0:T(8,128)}, u32[]{:S(2)}, u32[]{:S(2)}) collective-permute-start(f32[3,64,8,1]{1,2,3,0:T(8,128)} %copy.89), channel_id=1, source_target_pairs={{0,2},{2,4},{4,6},{6,0},{1,3},{3,5},{5,7},{7,1},{8,10},{10,12},{12... | collective-permute-start | bytes 18440 | tf_op jit(solution)/shard_map/ppermute | solution.py:59
  16.4 42.0 %collective-permute-start = (f32[3,64,8,1]{1,2,3,0:T(8,128)}, f32[3,64,8,1]{1,2,3,0:T(8,128)}, u32[]{:S(2)}, u32[]{:S(2)}) collective-permute-start(f32[3,64,8,1]{1,2,3,0:T(8,128)} %copy.88), channel_id=1, source_target_pairs={{2,0},{4,2},{6,4},{0,6},{3,1},{5,3},{7,5},{1,7},{10,8},{12,10},{14... | collective-permute-start | bytes 18440 | tf_op jit(solution)/shard_map/ppermute | solution.py:59
  27.2 16.6 %copy-start.31 = (f32[1,256]{1,0:T(1,128)}, f32[1,256]{1,0:T(1,128)S(1)}, u32[]{:S(2)}) copy-start(f32[1,256]{1,0:T(1,128)S(1)} %get-tuple-element.65) | copy-start | bytes 3076
  43.8 7.5 %copy-start.24 = (f32[64]{0:T(128)}, f32[64]{0:T(128)S(1)}, u32[]{:S(2)}) copy-start(f32[64]{0:T(128)S(1)} %fusion.69) | copy-start | bytes 772
  43.9 7.4 %copy-start.27 = (f32[64]{0:T(128)}, f32[64]{0:T(128)S(1)}, u32[]{:S(2)}) copy-start(f32[64]{0:T(128)S(1)} %fusion.68) | copy-start | bytes 772
  47.1 4.9 %copy-start.32 = (f32[1,256]{1,0:T(1,128)S(1)}, f32[1,256]{1,0:T(1,128)}, u32[]{:S(2)}) copy-start(f32[1,256]{1,0:T(1,128)} %copy-done.31) | copy-start | bytes 3076
  50.2 4.8 %copy-start.10 = (f32[64,8,128]{2,1,0:T(8,128)S(1)}, f32[64,8,128]{2,1,0:T(8,128)}, u32[]{:S(2)}) copy-start(f32[64,8,128]{2,1,0:T(8,128)} %get-tuple-element.48) | copy-start | bytes 786436
  54.9 8.4 %copy-start.4 = (f32[3,64,7,128]{3,1,2,0:T(8,128)S(1)}, f32[3,64,7,128]{3,1,2,0:T(8,128)}, u32[]{:S(2)}) copy-start(f32[3,64,7,128]{3,1,2,0:T(8,128)} %get-tuple-element.44) | copy-start | bytes 2064388
  63.3 3.5 %copy-start.11 = (f32[3,64,1,128]{3,1,2,0:T(8,128)}, f32[3,64,1,128]{3,1,2,0:T(8,128)S(1)}, u32[]{:S(2)}) copy-start(f32[3,64,1,128]{3,1,2,0:T(8,128)S(1)} %get-tuple-element.53) | copy-start | bytes 294916
  63.3 3.5 %copy-start.13 = (f32[3,64,1,128]{3,1,2,0:T(8,128)}, f32[3,64,1,128]{3,1,2,0:T(8,128)S(1)}, u32[]{:S(2)}) copy-start(f32[3,64,1,128]{3,1,2,0:T(8,128)S(1)} %get-tuple-element.54) | copy-start | bytes 294916
  81.2 4.3 %copy-start.3 = (bf16[512,2048]{1,0:T(8,128)(2,1)S(1)}, bf16[512,2048]{1,0:T(8,128)(2,1)}, u32[]{:S(2)}) copy-start(bf16[512,2048]{1,0:T(8,128)(2,1)} %copy-done.2) | copy-start | bytes 6291460
  97.0 5.5 %copy-start.15 = (f32[1,24,1024]{2,1,0:T(8,128)S(1)}, f32[1,24,1024]{2,1,0:T(8,128)}, u32[]{:S(2)}) copy-start(f32[1,24,1024]{2,1,0:T(8,128)} %convolution_bitcast_fusion) | copy-start | bytes 294916
  97.0 5.5 %copy-start.16 = (f32[1,24,1024]{2,1,0:T(8,128)S(1)}, f32[1,24,1024]{2,1,0:T(8,128)}, u32[]{:S(2)}) copy-start(f32[1,24,1024]{2,1,0:T(8,128)} %convolution_bitcast_fusion.1) | copy-start | bytes 294916
  97.8 98.5 %all-reduce.9.cloned.1.call-start = ((), (), s32[]{:S(2)}) async-start(), calls=%async_computation | async-start | bytes 393216 | tf_op jit(solution)/shard_map/psum | solution.py:179
  98.7 98.6 %collective-permute-start.5 = (f32[3,64,2,128]{3,1,2,0:T(8,128)}, f32[3,64,2,128]{3,1,2,0:T(8,128)}, u32[]{:S(2)}, u32[]{:S(2)}) collective-permute-start(f32[3,64,2,128]{3,1,2,0:T(8,128)} %pad_maximum_fusion.3), channel_id=1, source_target_pairs={{0,1},{1,0},{2,3},{3,2},{4,5},{5,4},{6,7},{7,6},{8,9},{9,8},{10,11... | collective-permute-start | bytes 589832 | tf_op jit(solution)/shard_map/ppermute | solution.py:56
  100.4 7.7 %collective-permute-start.3 = (f32[3,64,8,1]{1,2,3,0:T(8,128)S(1)}, f32[3,64,8,1]{1,2,3,0:T(8,128)S(1)}, u32[]{:S(2)}, u32[]{:S(2)}) collective-permute-start(f32[3,64,8,1]{1,2,3,0:T(8,128)S(1)} %copy.78), channel_id=1, source_target_pairs={{2,0},{4,2},{6,4},{0,6},{3,1},{5,3},{7,5},{1,7},{10,8},{12,10},{14... | collective-permute-start | bytes 18440 | tf_op jit(solution)/shard_map/ppermute | solution.py:59
  102.2 5.5 %collective-permute-start.4 = (f32[3,64,8,1]{1,2,3,0:T(8,128)S(1)}, f32[3,64,8,1]{1,2,3,0:T(8,128)S(1)}, u32[]{:S(2)}, u32[]{:S(2)}) collective-permute-start(f32[3,64,8,1]{1,2,3,0:T(8,128)S(1)} %copy.80), channel_id=1, source_target_pairs={{0,2},{2,4},{4,6},{6,0},{1,3},{3,5},{5,7},{7,1},{8,10},{10,12},{12... | collective-permute-start | bytes 18440 | tf_op jit(solution)/shard_map/ppermute | solution.py:59
  105.6 93.6 %copy-start.9 = (f32[64,8,128]{2,0,1:T(8,128)S(1)}, f32[64,8,128]{2,0,1:T(8,128)}, u32[]{:S(2)}) copy-start(f32[64,8,128]{2,0,1:T(8,128)} %get-tuple-element.24) | copy-start | bytes 786436
  105.6 93.6 %copy-start.26 = (f32[64]{0:T(128)S(1)}, f32[64]{0:T(128)}, u32[]{:S(2)}) copy-start(f32[64]{0:T(128)} %copy-done.24) | copy-start | bytes 772
  (19 other events, 49.9 us)
Sparse Core Ops, SparseCore 0:
  97.9 51.1 all-reduce.10
  152.3 43.9 all-reduce.8

commit v2 on v1

--- a/solution.py
+++ b/solution.py
@@ -34,6 +34,201 @@
     total_ref[...] = c + d * flux + end_ref[...] * value
 
 
+MESH = pl.DeviceIdType.MESH
+VMEM = pl.BlockSpec(memory_space=pltpu.VMEM)
+
+
+def gather_kernel(count, part_ref, out_ref, slots, send_sem, recv_sem):
+    me = lax.axis_index("line")
+    barrier = pltpu.get_barrier_semaphore()
+    for k in range(1, count):
+        pl.semaphore_signal(
+            barrier, inc=1, device_id={"line": lax.rem(me + k, count)}, device_id_type=MESH
+        )
+    pl.semaphore_wait(barrier, count - 1)
+    copies = []
+    for k in range(1, count):
+        copy = pltpu.make_async_remote_copy(
+            src_ref=part_ref,
+            dst_ref=slots.at[k],
+            send_sem=send_sem.at[k],
+            recv_sem=recv_sem.at[k],
+            device_id={"line": lax.rem(me + k, count)},
+            device_id_type=MESH,
+        )
+        copy.start()
+        copies.append(copy)
+    out_ref[pl.ds(me, 1)] = part_ref[...][None]
+    for k in range(1, count):
+        copies[k - 1].wait_recv()
+        out_ref[pl.ds(lax.rem(me + count - k, count), 1)] = slots[k][None]
+    for copy in copies:
+        copy.wait_send()
+
+
+def line_gather(part, collective_id):
+    count = lax.axis_size("line")
+    return pl.pallas_call(
+        lambda *refs: gather_kernel(count, *refs),
+        out_shape=jax.ShapeDtypeStruct((count,) + part.shape, part.dtype),
+        in_specs=[VMEM],
+        out_specs=VMEM,
+        scratch_shapes=[
+            pltpu.VMEM((count,) + part.shape, part.dtype),
+            pltpu.SemaphoreType.DMA((count,)),
+            pltpu.SemaphoreType.DMA((count,)),
+        ],
+        compiler_params=pltpu.CompilerParams(
+            collective_id=collective_id, has_side_effects=True, vmem_limit_bytes=32 * 2**20
+        ),
+        name="line_gather",
+    )(part)
+
+
+def sum_kernel(
+    lines,
+    streams,
+    spans,
+    part_ref,
+    slab_ref,
+    total_ref,
+    wall_ref,
+    arrived,
+    whole,
+    walls,
+    scatter_send,
+    scatter_recv,
+    spread_send,
+    spread_recv,
+    wall_send,
+    wall_recv,
+):
+    group = streams * spans
+    chunk = part_ref.shape[0] // group
+    line = lax.axis_index("line")
+    me = lax.axis_index("stream") * spans + lax.axis_index("span")
+
+    def member(k):
+        other = lax.rem(me + k, group)
+        return other, {"stream": other // spans, "span": lax.rem(other, spans)}
+
+    def rows(index):
+        return pl.ds(pl.multiple_of(index * chunk, 8), chunk)
+
+    barrier = pltpu.get_barrier_semaphore()
+    for k in range(1, group):
+        pl.semaphore_signal(barrier, inc=1, device_id=member(k)[1], device_id_type=MESH)
+    for k in range(1, lines):
+        pl.semaphore_signal(
+            barrier, inc=1, device_id={"line": lax.rem(line + k, lines)}, device_id_type=MESH
+        )
+    pl.semaphore_wait(barrier, group + lines - 2)
+
+    scatter = []
+    for k in range(1, group):
+        other, device = member(k)
+        copy = pltpu.make_async_remote_copy(
+            src_ref=part_ref.at[rows(other)],
+            dst_ref=arrived.at[k],
+            send_sem=scatter_send.at[k],
+            recv_sem=scatter_recv.at[k],
+            device_id=device,
+            device_id_type=MESH,
+        )
+        copy.start()
+        scatter.append(copy)
+
+    def wall_copy(wall, slot, target):
+        return pltpu.make_async_remote_copy(
+            src_ref=slab_ref.at[wall],
+            dst_ref=walls.at[slot],
+            send_sem=wall_send.at[wall],
+            recv_sem=wall_recv.at[slot],
+            device_id={"line": target},
+            device_id_type=MESH,
+        )
+
+    ends = (0, lines - 1)
+    for wall, target in enumerate(ends):
+
+        @pl.when(line != target)
+        def _(wall=wall, target=target):
+            wall_copy(wall, lax.rem(line - target + lines, lines), target).start()
+
+    own = part_ref[rows(me)]
+    for k in range(1, group):
+        scatter[k - 1].wait_recv()
+        own = own + arrived[k]
+    whole[rows(me)] = own
+    spread = []
+    for k in range(1, group):
+        copy = pltpu.make_async_remote_copy(
+            src_ref=whole.at[rows(me)],
+            dst_ref=whole.at[rows(me)],
+            send_sem=spread_send.at[k],
+            recv_sem=spread_recv.at[k],
+            device_id=member(k)[1],
+            device_id_type=MESH,
+        )
+        copy.start()
+        spread.append(copy)
+
+    wall_ref[...] = jnp.zeros_like(wall_ref)
+    for wall, target in enumerate(ends):
+
+        @pl.when(line == target)
+        def _(wall=wall, target=target):
+            added = slab_ref[wall]
+            for k in range(1, lines):
+                wall_copy(wall, k, lax.rem(line + 1, lines)).wait_recv()
+                added = added + walls[k]
+            wall_ref[...] = added
+
+        @pl.when(line != target)
+        def _(wall=wall, target=target):
+            wall_copy(wall, lax.rem(line - target + lines, lines), target).wait_send()
+
+    for copy in spread:
+        copy.wait_recv()
+    total_ref[...] = whole[...]
+    for copy in scatter + spread:
+        copy.wait_send()
+
+
+def group_sum(part, slabs):
+    lines, streams, spans = (lax.axis_size(a) for a in ("line", "stream", "span"))
+    group = streams * spans
+    height = part.shape[0]
+    padded = -(-height // (8 * group)) * (8 * group)
+    part = jnp.pad(part, ((0, padded - height), (0, 0)))
+    dma = pltpu.SemaphoreType.DMA
+    total, wall = pl.pallas_call(
+        lambda *refs: sum_kernel(lines, streams, spans, *refs),
+        out_shape=(
+            jax.ShapeDtypeStruct(part.shape, jnp.float32),
+            jax.ShapeDtypeStruct(slabs.shape[1:], jnp.float32),
+        ),
+        in_specs=[VMEM, VMEM],
+        out_specs=(VMEM, VMEM),
+        scratch_shapes=[
+            pltpu.VMEM((group, padded // group, part.shape[1]), jnp.float32),
+            pltpu.VMEM(part.shape, jnp.float32),
+            pltpu.VMEM((lines,) + slabs.shape[1:], jnp.float32),
+            dma((group,)),
+            dma((group,)),
+            dma((group,)),
+            dma((group,)),
+            dma((2,)),
+            dma((lines,)),
+        ],
+        compiler_params=pltpu.CompilerParams(
+            collective_id=2, has_side_effects=True, vmem_limit_bytes=32 * 2**20
+        ),
+        name="group_sum",
+    )(part, slabs)
+    return total[:height], wall
+
+
 def green_factors(diffusion):
     count = diffusion.shape[0]
     faces = jnp.concatenate([diffusion, diffusion[-1:]])
@@ -79,7 +274,7 @@
     slab_bottom = velocity[:, :WALL_ROWS]
     slab_top = velocity[:, row_count - WALL_ROWS :][:, ::-1]
     own_slab = jnp.where(at_top, slab_top, slab_bottom).reshape(3 * WALL_ROWS, columns)
-    slabs = lax.all_gather(own_slab, "line")
+    slabs = line_gather(own_slab, 0)
     walls = (slabs[0], slabs[line_count - 1])
 
     low, high, scale = green_factors(diffusion)
@@ -122,7 +317,8 @@
     solved = jnp.einsum("ij,cjzx->cizx", operator, both, precision=HIGHEST)
     sums = solved[:, row_count:].reshape(12, columns)
     stress_part = stress_part.reshape(3, 2, columns).reshape(6, columns)
-    gathered = lax.all_gather(jnp.concatenate([sums, stress_part]), "line")
+    fill = jnp.zeros((6, columns), jnp.float32)
+    gathered = line_gather(jnp.concatenate([sums, stress_part, fill]), 1)
     part = gathered[:, :12].reshape(line_count, 6, 2, planes, cells)
     place = jnp.arange(line_count)
     below = (place < line_index).astype(jnp.float32)
@@ -130,7 +326,7 @@
     sum_below = jnp.sum(part[:, :, 0] * below[:, None, None, None], axis=0) * scale
     sum_above = jnp.sum(part[:, :, 1] * above[:, None, None, None], axis=0) * scale
     mask_float = wall_mask.astype(jnp.float32)
-    stress = jnp.sum(gathered[:, 12:], axis=0).reshape(3, 2, planes, cells) * mask_float[None]
+    stress = jnp.sum(gathered[:, 12:18], axis=0).reshape(3, 2, planes, cells) * mask_float[None]
     from_low = sum_below[:3] + stress[:, 0] * (low[0] * scale)
     from_high = sum_above[:3] + stress[:, 1] * (high[all_rows - 1] * scale)
     low_col, high_col = low_own[None, :, None, None], high_own[None, :, None, None]
@@ -153,14 +349,13 @@
     )
     hidden_float = hidden.astype(jnp.float32)
     pre_grad = (hidden_grad * (1.0 - hidden_float * hidden_float)).astype(jnp.bfloat16)
-    wide = jnp.concatenate([features, jnp.ones((1, 2 * columns), jnp.bfloat16)])
-    grad_in = lax.dot_general(
-        pre_grad, wide, (((1,), (1,)), ((), ())), preferred_element_type=jnp.float32
-    )
-    grad_out = lax.dot_general(
-        hidden, stress_grad, (((1,), (1,)), ((), ())), preferred_element_type=jnp.float32
-    )
-    totals = lax.psum(jnp.concatenate([grad_in, grad_out], axis=1), ("stream", "span"))
+    contract = (((1,), (1,)), ((), ()))
+    grad_in = lax.dot_general(pre_grad, features, contract, preferred_element_type=jnp.float32)
+    grad_out = lax.dot_general(stress_grad, hidden, contract, preferred_element_type=jnp.float32)
+    ones = jnp.ones((1, 2 * columns), jnp.bfloat16)
+    grad_bias = lax.dot_general(ones, pre_grad, contract, preferred_element_type=jnp.float32)
+    extra = jnp.concatenate([grad_out, grad_bias, jnp.zeros((4, share), jnp.float32)])
+    extra_rows = 8 * share // feature_count
 
     feature_grad = lax.dot_general(
         weight_in, pre_grad, (((0,), (0,)), ((), ())), preferred_element_type=jnp.float32
@@ -176,9 +371,9 @@
             for w in range(2)
         ]
     )
-    slab_sum = lax.psum(slab_part, "line")
-    at_wall = jnp.logical_or(line_index == 0, at_top)
-    slab_grad = jnp.where(at_top, slab_sum[1], slab_sum[0]) * at_wall.astype(jnp.float32)
+    packed = jnp.concatenate([grad_in, extra.reshape(extra_rows, feature_count)])
+    totals, slab_grad = group_sum(packed, slab_part)
+    extra_total = totals[share:].reshape(8, share)
     slab_grad = slab_grad.reshape(3, WALL_ROWS, planes, cells)
 
     flux_stream = velocity[0] * multiplier
@@ -200,9 +395,9 @@
     return (
         new_velocity,
         adjoint,
-        totals[:, :feature_count],
-        totals[:, feature_count],
-        jnp.transpose(totals[:, feature_count + 1 :]),
+        totals[:share],
+        extra_total[3],
+        extra_total[:3],
     )
 
 

time: 211 us -> 121 us (0.57)
  waiting for transfers between devices: 83.1 us -> 1.12 us
  Pallas kernels: 1.85 us -> 33.2 us
  blocking collectives: 19.2 us -> 0 us
  between operations: 16.6 us -> 3.38 us
  other arithmetic: 20.4 us -> 13.9 us
  local copies, waits for them, and re-layouts: 48.6 us -> 44.2 us
  starting transfers between devices: 7.37 us -> 10.3 us
    psum x2 -> x0, waiting for transfers between devices: 80.9 us -> none  [the longest x1 41.1 us: local(): slab_sum = lax.psum(slab_part, 'line')]
    pallas_call x0 -> x3, Pallas kernels: none -> 31.3 us  [the longest x2 16 us: line_gather(): pl.pallas_call(lambda *refs: gather_kernel(count, *refs), out_shape=jax.S...]
    all_gather x2 -> x0, blocking collectives: 19.2 us -> none  [the longest x1 9.74 us: local(): slabs = lax.all_gather(own_slab, 'line')]
    ppermute x2, starting transfers between devices: 3.87 us -> 6.43 us  [halos(): lax.ppermute(first, axis, [(j, i) for i, j in up])]
    concatenate x2 -> x3, other arithmetic: 2.52 us -> 0.17 us  [the longest x1 0.08 us: local(): gathered = line_gather(jnp.concatenate([sums, stress_part, fill]), 1)]
    unnamed x80 -> x95, local copies, waits for them, and re-layouts: 13.6 us -> 11.8 us
    dot_general x2 -> x3, matrix products: 3.07 us -> 4.43 us  [the longest x1 2.37 us: local(): lax.dot_general(stress_grad, hidden, contract, preferred_element_type=jnp...]
  transfers between devices with their start and end apart: 8 -> 6, of which waited for: 3 -> 1; matrix products, arithmetic and copies ran while one was open for 22% -> 34% of each run, Pallas kernels for 1% -> 8%
where the time goes in v2:
time: 121 us
  local copies, waits for them, and re-layouts  44.2 us (37%)
  Pallas kernels  33.2 us (27%)
  matrix products  14.6 us (12%)
  other arithmetic  13.9 us (11%)
  starting transfers between devices  10.3 us (9%)
  between operations  3.38 us (3%)
    pallas_call x2, Pallas kernels, line_gather(): pl.pallas_call(lambda *refs: gather_kernel(count, *refs), out_shape=jax.S...  16 us
    pallas_call x1, Pallas kernels, group_sum(): pl.pallas_call(lambda *refs: sum_kernel(lines, streams, spans, *refs), ou...  15.3 us
    unnamed x95, local copies, waits for them, and re-layouts  11.8 us
    ppermute x2, starting transfers between devices, halos(): lax.ppermute(first, axis, [(j, i) for i, j in up])  6.43 us
    sub x1, other arithmetic, local(): velocity - ADVECT * (velocity[0] * grad_stream + velocity[2] * grad_span)  3.36 us
    slice x4, local copies, waits for them, and re-layouts, halos(): first = lax.slice_in_dim(shard, 0, 1, axis=dim)  3.25 us
    slice x2, local copies, waits for them, and re-layouts, halos(): last = lax.slice_in_dim(shard, length - 1, length, axis=dim)  2.81 us
    add x1, other arithmetic, local(): adjoint + own  2.73 us
  transfers between devices with their start and end apart: 6, of which 1 were waited for; matrix products, arithmetic and copies ran while one was open for 34% of the time, Pallas kernels for 8%

profile of v2, /device:TPU:0, one launch (start us, length us, event | category | flops | bytes accessed | tf_op | source)
XLA Modules:
  0.0 120.6 jit_solution(8493793722075268818)
XLA Ops:
  4.3 2.0 %copy.87 = f32[3,64,8,1]{1,2,3,0:T(8,128)} copy(f32[3,64,8,1]{3,2,1,0:T(8,128)} %get-tuple-element.46) | data formatting | bytes 12288
  6.4 2.6 %collective-permute-start.1 = (f32[3,64,8,1]{1,2,3,0:T(8,128)}, f32[3,64,8,1]{1,2,3,0:T(8,128)}, u32[]{:S(2)}, u32[]{:S(2)}) collective-permute-start(f32[3,64,8,1]{1,2,3,0:T(8,128)} %copy.87), channel_id=1, source_target_pairs={{0,2},{2,4},{4,6},{6,0},{1,3},{3,5},{5,7},{7,1},{8,10},{10,12},{12... | collective-permute-start | bytes 18440 | tf_op jit(solution)/shard_map/ppermute | solution.py:254
  9.9 2.0 %collective-permute-start = (f32[3,64,8,1]{1,2,3,0:T(8,128)}, f32[3,64,8,1]{1,2,3,0:T(8,128)}, u32[]{:S(2)}, u32[]{:S(2)}) collective-permute-start(f32[3,64,8,1]{1,2,3,0:T(8,128)} %copy.86), channel_id=1, source_target_pairs={{2,0},{4,2},{6,4},{0,6},{3,1},{5,3},{7,5},{1,7},{10,8},{12,10},{14... | collective-permute-start | bytes 18440 | tf_op jit(solution)/shard_map/ppermute | solution.py:254
  16.6 1.9 %green.1 = (f32[8,256]{1,0:T(8,128)}, f32[8,256]{1,0:T(8,128)}) custom-call(f32[8,256]{1,0:T(8,128)} %pad.26.step_ref, f32[8,256]{1,0:T(8,128)} %pad.28.start_ref, f32[8,256]{1,0:T(8,128)} %pad.30.end_ref), custom_call_target="tpu_custom_call" | custom-call | tf_op jit(solution)/shard_map/green/pallas_call | solution.py:240
  22.2 8.2 %line_gather.2 = f32[4,24,1024]{2,1,0:T(8,128)S(1)} custom-call(f32[24,1024]{1,0:T(8,128)S(1)} %fusion.20.refs_0_), custom_call_target="tpu_custom_call" | custom-call | tf_op jit(solution)/shard_map/line_gather/pallas_call | solution.py:71
  32.7 1.6 %fusion.59 = (f32[3,64,8,127]{3,1,2,0:T(8,128)}, f32[3,64,8,127]{3,1,2,0:T(8,128)}) fusion(f32[3,64,8,128]{3,1,2,0:T(8,128)S(1)} %copy.67), kind=kLoop, calls=%fused_computation.114 | loop fusion | bytes 3121152 | tf_op jit(solution)/shard_map/slice | solution.py:260
  37.4 1.8 %tanh_convert_fusion = bf16[512,2048]{1,0:T(8,128)(2,1)S(1)} fusion(f32[512]{0:T(512)S(1)} %dynamic_slice.19, bf16[128,1024]{1,0:T(8,128)(2,1)} %convolution_convert_fusion, bf16[128,1024]{1,0:T(8,128)(2,1)} %convolution_convert_fusion.1, bf16[2048,128]{1,0:T(8,128)(2,1)S(1)} %copy-done, s32[]{:T(128)S(6)} %select_n.35), kind=kOutput, calls=%fused_computation.1 | convolution fusion | flops 271581184 | bytes 2754564 | tf_op jit(solution)/shard_map/dot_general | solution.py:312
  47.9 2.2 %copy.68 = f32[3,64,8,128]{3,1,2,0:T(8,128)} copy(f32[3,64,8,128]{3,2,1,0:T(8,128)} %param.9) | data formatting | bytes 1572864 | tf_op args[1]
  51.7 1.9 %copy.61 = f32[3,64,8,1]{3,1,2,0:T(8,128)} copy(f32[3,64,8,1]{1,2,3,0:T(8,128)} %collective-permute-done.1) | data formatting | bytes 12288 | tf_op jit(solution)/shard_map/ppermute | solution.py:254
  54.6 3.4 %multiply_subtract_fusion = (f32[3,64,8,128]{3,1,2,0:T(8,128)S(1)}, f32[3,64,8,128]{3,1,2,0:T(8,128)}) fusion(f32[64,8,128]{2,0,1:T(8,128)} %copy.62, f32[64,8,128]{2,0,1:T(8,128)} %copy.55, f32[3,64,7,128]{3,1,2,0:T(8,128)S(1)} %get-tuple-element.48, f32[3,64,1,128]{3,1,2,0:T(8,128)S(1)} %get-tuple-element.58, f32[3,64,1,128]{3,1,2,0:T(8,128)S(1)} %get-tuple-element.57, ...), kind=kLoop, calls=%fused_computation.27 | loop fusion | flops 2162688 | bytes 6029312 | tf_op jit(solution)/shard_map/sub | solution.py:297
  58.0 1.7 %fusion.4 = f32[6,66,8,128]{3,1,2,0:T(8,128)S(1)} fusion(f32[3,64,8,128]{3,1,2,0:T(8,128)S(1)} %copy-done.8, f32[3,64,8,128]{3,1,2,0:T(8,128)S(1)} %get-tuple-element.30, f32[1,64]{0,1:T(8,128)S(1)} %copy-done.23, f32[1,64]{0,1:T(8,128)S(1)} %copy-done.22, f32[64,64]{0,1:T(8,128)S(1)} %select_multiply_fusion), kind=kOutput, calls=%fused_computation.6 | convolution fusion | flops 311828736 | bytes 3211776 | tf_op jit(solution)/shard_map/ij,cjzx->cizx/dot_general | solution.py:317
  59.9 7.8 %line_gather.3 = f32[4,24,1024]{2,1,0:T(8,128)S(1)} custom-call(f32[24,1024]{1,0:T(8,128)S(1)} %maximum_maximum_fusion.refs_0_), custom_call_target="tpu_custom_call" | custom-call | tf_op jit(solution)/shard_map/line_gather/pallas_call | solution.py:71
  67.9 2.4 %fusion.48 = f32[3,512]{1,0:T(4,128)S(1)} fusion(bf16[512,2048]{1,0:T(8,128)(2,1)} %copy-done.2, f32[1,3,16,128]{3,2,1,0:T(8,128)S(1)} %maximum_bitcast_fusion.2, f32[2048]{0:T(1024)S(1)} %get-tuple-element.65), kind=kOutput, calls=%fused_computation.104 | convolution fusion | flops 6303744 | bytes 2136064 | tf_op jit(solution)/shard_map/dot_general | solution.py:354
  70.3 1.7 %multiply_convert_fusion = bf16[512,2048]{1,0:T(8,128)(2,1)S(1)} fusion(bf16[512,2048]{1,0:T(8,128)(2,1)S(1)} %copy-done.3, bf16[3,2048]{1,0:T(4,128)(2,1)} %param.12, s32[]{:T(128)S(6)} %select_n.35, f32[1,3,16,128]{3,2,1,0:T(8,128)S(1)} %maximum_bitcast_fusion.2, f32[2048]{0:T(1024)S(1)} %get-tuple-element.65), kind=kOutput, calls=%fused_computation | convolution fusion | flops 11546624 | bytes 4231172 | tf_op jit(solution)/shard_map/dot_general | solution.py:347
  72.0 1.4 %fusion.16 = f32[512,128]{1,0:T(8,128)} fusion(bf16[512,2048]{1,0:T(8,128)(2,1)S(1)} %multiply_convert_fusion, bf16[128,1024]{1,0:T(8,128)(2,1)S(1)} %copy-done.19, bf16[128,1024]{1,0:T(8,128)(2,1)S(1)} %copy-done.20), kind=kOutput, calls=%fused_computation.33 | convolution fusion | flops 269484032 | bytes 2883584 | tf_op jit(solution)/shard_map/dot_general | solution.py:353
  76.2 2.3 %multiply_reduce_fusion.1 = (f32[64,8,128]{2,0,1:T(8,128)S(1)}, f32[64,8,128]{2,0,1:T(8,128)}, f32[3,64,8,128]{3,1,2,0:T(8,128)S(1)}, f32[3,64,8,128]{3,1,2,0:T(8,128)S(1)}, f32[3,64,8,128]{3,1,2,0:T(8,128)}) fusion(f32[3,64,8,128]{3,1,2,0:T(8,128)S(1)} %copy-done.9, f32[3,8,128]{2,1,0:T(8,128)S(1)} %get-tuple-element.64, f32[64]{0:T(128)S(1)} %copy-done.32, ...), kind=kLoop, calls=%fused_computation.26 | loop fusion | flops 3211264 | bytes 7389696 | tf_op jit(solution)/shard_map/reduce_sum | solution.py:386
  80.4 1.4 %fusion.58 = (f32[3,64,8,127]{3,1,2,0:T(8,128)}, f32[3,64,8,127]{3,1,2,0:T(8,128)}) fusion(f32[3,64,8,128]{3,1,2,0:T(8,128)S(1)} %get-tuple-element.33), kind=kLoop, calls=%fused_computation.113 | loop fusion | bytes 3121152 | tf_op jit(solution)/shard_map/slice | solution.py:261
  83.4 15.3 %group_sum.1 = (f32[576,128]{1,0:T(8,128)S(1)}, f32[24,1024]{1,0:T(8,128)S(1)}) custom-call(f32[576,128]{1,0:T(8,128)S(1)} %select_maximum_fusion.refs_0_, f32[2,24,1024]{2,1,0:T(8,128)S(1)} %pad_maximum_fusion.5.refs_1_), custom_call_target="tpu_custom_call" | custom-call | tf_op jit(solution)/shard_map/group_sum/pallas_call | solution.py:205
  98.8 1.6 %pad_maximum_fusion.4 = f32[3,64,2,128]{3,1,2,0:T(8,128)} fusion(f32[3,64,1,128]{3,1,2,0:T(8,128)} %get-tuple-element.38, f32[3,64,1,128]{3,1,2,0:T(8,128)S(1)} %get-tuple-element.37), kind=kLoop, calls=%fused_computation.39 | loop fusion | flops 49152 | bytes 393216 | tf_op jit(solution)/shard_map/concatenate | solution.py:251
  101.2 1.4 %copy.79 = f32[3,64,8,1]{1,2,3,0:T(8,128)S(1)} copy(f32[3,64,8,1]{3,1,2,0:T(8,128)} %get-tuple-element.39) | data formatting | bytes 12288 | tf_op jit(solution)/shard_map/slice | solution.py:248
  102.6 1.4 %copy.77 = f32[3,64,8,1]{1,2,3,0:T(8,128)S(1)} copy(f32[3,64,8,1]{3,1,2,0:T(8,128)} %get-tuple-element.40) | data formatting | bytes 12288 | tf_op jit(solution)/shard_map/slice | solution.py:249
  104.1 4.4 %collective-permute-start.3 = (f32[3,64,8,1]{1,2,3,0:T(8,128)S(1)}, f32[3,64,8,1]{1,2,3,0:T(8,128)S(1)}, u32[]{:S(2)}, u32[]{:S(2)}) collective-permute-start(f32[3,64,8,1]{1,2,3,0:T(8,128)S(1)} %copy.77), channel_id=1, source_target_pairs={{2,0},{4,2},{6,4},{0,6},{3,1},{5,3},{7,5},{1,7},{10,8},{12,10},{14... | collective-permute-start | bytes 18440 | tf_op jit(solution)/shard_map/ppermute | solution.py:254
  110.4 2.5 %copy.82 = f32[3,64,8,128]{3,2,1,0:T(8,128)} copy(f32[3,64,8,128]{3,1,2,0:T(8,128)} %get-tuple-element.34) | data formatting | bytes 1572864
  116.5 2.7 %fusion.13 = f32[3,64,8,128]{3,1,2,0:T(8,128)S(1)} fusion(f32[3,64,8,1]{3,1,2,0:T(8,128)} %copy.78, f32[3,64,8,127]{3,1,2,0:T(8,128)} %get-tuple-element.42, f32[3,64,8,127]{3,1,2,0:T(8,128)} %get-tuple-element.41, f32[3,64,8,1]{3,1,2,0:T(8,128)S(1)} %copy.80, f32[3,64,1,128]{3,1,2,0:T(8,128)S(1)} %get-tuple-element.54, ...), kind=kLoop, calls=%fused_computation.22 | loop fusion | flops 3735552 | bytes 5366285 | tf_op jit(solution)/shard_map/add | solution.py:394
  (182 shorter events, 41.7 us)
Async XLA Ops:
  0.6 36.7 %copy-start = (bf16[2048,128]{1,0:T(8,128)(2,1)S(1)}, bf16[2048,128]{1,0:T(8,128)(2,1)}, u32[]{:S(2)}) copy-start(bf16[2048,128]{1,0:T(8,128)(2,1)} %param.10) | copy-start | bytes 1572868
  2.7 9.2 %copy-start.27 = (f32[256]{0:T(256)S(1)}, f32[256]{0:T(256)}, u32[]{:S(2)}) copy-start(f32[256]{0:T(256)} %param.13) | copy-start | bytes 3076
  2.7 50.9 %collective-permute-start.2 = (f32[3,64,2,128]{3,1,2,0:T(8,128)}, f32[3,64,2,128]{3,1,2,0:T(8,128)}, u32[]{:S(2)}, u32[]{:S(2)}) collective-permute-start(f32[3,64,2,128]{3,1,2,0:T(8,128)} %pad_maximum_fusion.3), channel_id=1, source_target_pairs={{0,1},{1,0},{2,3},{3,2},{4,5},{5,4},{6,7},{7,6},{8,9},{9,8},{10,11... | collective-permute-start | bytes 589832 | tf_op jit(solution)/shard_map/ppermute | solution.py:251
  4.3 17.7 %copy-start.35 = (s32[2,128]{1,0:T(2,128)S(1)}, s32[2,128]{1,0:T(2,128)}, u32[]{:S(2)}) copy-start(s32[2,128]{1,0:T(2,128)} %param.14) | copy-start | bytes 3076
  6.4 45.3 %collective-permute-start.1 = (f32[3,64,8,1]{1,2,3,0:T(8,128)}, f32[3,64,8,1]{1,2,3,0:T(8,128)}, u32[]{:S(2)}, u32[]{:S(2)}) collective-permute-start(f32[3,64,8,1]{1,2,3,0:T(8,128)} %copy.87), channel_id=1, source_target_pairs={{0,2},{2,4},{4,6},{6,0},{1,3},{3,5},{5,7},{7,1},{8,10},{10,12},{12... | collective-permute-start | bytes 18440 | tf_op jit(solution)/shard_map/ppermute | solution.py:254
  9.9 40.8 %collective-permute-start = (f32[3,64,8,1]{1,2,3,0:T(8,128)}, f32[3,64,8,1]{1,2,3,0:T(8,128)}, u32[]{:S(2)}, u32[]{:S(2)}) collective-permute-start(f32[3,64,8,1]{1,2,3,0:T(8,128)} %copy.86), channel_id=1, source_target_pairs={{2,0},{4,2},{6,4},{0,6},{3,1},{5,3},{7,5},{1,7},{10,8},{12,10},{14... | collective-permute-start | bytes 18440 | tf_op jit(solution)/shard_map/ppermute | solution.py:254
  20.6 15.2 %copy-start.36 = (f32[1,256]{1,0:T(1,128)}, f32[1,256]{1,0:T(1,128)S(1)}, u32[]{:S(2)}) copy-start(f32[1,256]{1,0:T(1,128)S(1)} %get-tuple-element.69) | copy-start | bytes 3076
  22.2 52.5 %copy-start.18 = (pred[2,128,24]{2,1,0:T(32,128)(4,1)}, pred[2,128,24]{2,1,0:T(32,128)(4,1)S(1)}, u32[]{:S(2)}) copy-start(pred[2,128,24]{2,1,0:T(32,128)(4,1)S(1)} %iota_compare_fusion.1) | copy-start | bytes 18436
  32.7 21.9 %copy-start.4 = (f32[3,64,7,128]{3,1,2,0:T(8,128)}, f32[3,64,7,128]{3,1,2,0:T(8,128)S(1)}, u32[]{:S(2)}) copy-start(f32[3,64,7,128]{3,1,2,0:T(8,128)S(1)} %get-tuple-element.47) | copy-start | bytes 2064388
  32.7 21.9 %copy-start.6 = (f32[3,64,7,128]{3,1,2,0:T(8,128)}, f32[3,64,7,128]{3,1,2,0:T(8,128)S(1)}, u32[]{:S(2)}) copy-start(f32[3,64,7,128]{3,1,2,0:T(8,128)S(1)} %get-tuple-element.48) | copy-start | bytes 2064388
  35.8 5.8 %copy-start.28 = (f32[64]{0:T(128)}, f32[64]{0:T(128)S(1)}, u32[]{:S(2)}) copy-start(f32[64]{0:T(128)S(1)} %fusion.76) | copy-start | bytes 772
  35.9 5.8 %copy-start.31 = (f32[64]{0:T(128)}, f32[64]{0:T(128)S(1)}, u32[]{:S(2)}) copy-start(f32[64]{0:T(128)S(1)} %fusion.75) | copy-start | bytes 772
  37.4 4.5 %copy-start.37 = (f32[1,256]{1,0:T(1,128)S(1)}, f32[1,256]{1,0:T(1,128)}, u32[]{:S(2)}) copy-start(f32[1,256]{1,0:T(1,128)} %copy-done.36) | copy-start | bytes 3076
  37.4 9.0 %copy-start.13 = (f32[64,8,128]{2,1,0:T(8,128)S(1)}, f32[64,8,128]{2,1,0:T(8,128)}, u32[]{:S(2)}) copy-start(f32[64,8,128]{2,1,0:T(8,128)} %get-tuple-element.51) | copy-start | bytes 786436
  40.5 6.6 %copy-start.12 = (f32[64,8,128]{2,1,0:T(8,128)S(1)}, f32[64,8,128]{2,1,0:T(8,128)}, u32[]{:S(2)}) copy-start(f32[64,8,128]{2,1,0:T(8,128)} %get-tuple-element.52) | copy-start | bytes 786436
  54.6 3.4 %copy-start.14 = (f32[3,64,1,128]{3,1,2,0:T(8,128)}, f32[3,64,1,128]{3,1,2,0:T(8,128)S(1)}, u32[]{:S(2)}) copy-start(f32[3,64,1,128]{3,1,2,0:T(8,128)S(1)} %get-tuple-element.57) | copy-start | bytes 294916
  54.6 3.4 %copy-start.16 = (f32[3,64,1,128]{3,1,2,0:T(8,128)}, f32[3,64,1,128]{3,1,2,0:T(8,128)S(1)}, u32[]{:S(2)}) copy-start(f32[3,64,1,128]{3,1,2,0:T(8,128)S(1)} %get-tuple-element.58) | copy-start | bytes 294916
  100.4 15.2 %collective-permute-start.5 = (f32[3,64,2,128]{3,1,2,0:T(8,128)}, f32[3,64,2,128]{3,1,2,0:T(8,128)}, u32[]{:S(2)}, u32[]{:S(2)}) collective-permute-start(f32[3,64,2,128]{3,1,2,0:T(8,128)} %pad_maximum_fusion.4), channel_id=1, source_target_pairs={{0,1},{1,0},{2,3},{3,2},{4,5},{5,4},{6,7},{7,6},{8,9},{9,8},{10,11... | collective-permute-start | bytes 589832 | tf_op jit(solution)/shard_map/ppermute | solution.py:251
  104.0 12.4 %copy-start.26 = (f32[3,8,128]{2,1,0:T(8,128)S(1)}, f32[3,8,128]{2,1,0:T(8,128)}, u32[]{:S(2)}) copy-start(f32[3,8,128]{2,1,0:T(8,128)} %copy-done.25) | copy-start | bytes 36868
  104.0 12.4 %copy-start.30 = (f32[64]{0:T(128)S(1)}, f32[64]{0:T(128)}, u32[]{:S(2)}) copy-start(f32[64]{0:T(128)} %copy-done.28) | copy-start | bytes 772
  104.0 12.5 %copy-start.33 = (f32[64]{0:T(128)S(1)}, f32[64]{0:T(128)}, u32[]{:S(2)}) copy-start(f32[64]{0:T(128)} %copy-done.31) | copy-start | bytes 772
  104.1 12.4 %copy-start.38 = (f32[3]{0:T(128)S(1)}, f32[3]{0:T(128)}, u32[]{:S(2)}) copy-start(f32[3]{0:T(128)} %pad.44.clone) | copy-start | bytes 40
  104.1 10.2 %collective-permute-start.3 = (f32[3,64,8,1]{1,2,3,0:T(8,128)S(1)}, f32[3,64,8,1]{1,2,3,0:T(8,128)S(1)}, u32[]{:S(2)}, u32[]{:S(2)}) collective-permute-start(f32[3,64,8,1]{1,2,3,0:T(8,128)S(1)} %copy.77), channel_id=1, source_target_pairs={{2,0},{4,2},{6,4},{0,6},{3,1},{5,3},{7,5},{1,7},{10,8},{12,10},{14... | collective-permute-start | bytes 18440 | tf_op jit(solution)/shard_map/ppermute | solution.py:254
  108.5 5.5 %collective-permute-start.4 = (f32[3,64,8,1]{1,2,3,0:T(8,128)S(1)}, f32[3,64,8,1]{1,2,3,0:T(8,128)S(1)}, u32[]{:S(2)}, u32[]{:S(2)}) collective-permute-start(f32[3,64,8,1]{1,2,3,0:T(8,128)S(1)} %copy.79), channel_id=1, source_target_pairs={{0,2},{2,4},{4,6},{6,0},{1,3},{3,5},{5,7},{7,1},{8,10},{10,12},{12... | collective-permute-start | bytes 18440 | tf_op jit(solution)/shard_map/ppermute | solution.py:254
  (25 other events, 55.1 us)

commit v3 on v2

--- a/solution.py
+++ b/solution.py
@@ -229,6 +229,170 @@
     return total[:height], wall
 
 
+def exchange(streams, spans, stream_part, span_part, refs):
+    edge_out, edge_in, plane_out, plane_in, spread, send_sem, recv_sem = refs
+    cells = spread.shape[2]
+    stream, span = lax.axis_index("stream"), lax.axis_index("span")
+    right = {"stream": lax.rem(stream + 1, streams)}
+    left = {"stream": lax.rem(stream + streams - 1, streams)}
+    after = {"span": lax.rem(span + 1, spans)}
+    before = {"span": lax.rem(span + spans - 1, spans)}
+    barrier = pltpu.get_barrier_semaphore()
+    for device in (right, left, after, before):
+        pl.semaphore_signal(barrier, inc=1, device_id=device, device_id_type=MESH)
+
+    def hot(height, first, second):
+        row = lax.broadcasted_iota(jnp.int32, (height, cells), 0)
+        lane = lax.broadcasted_iota(jnp.int32, (height, cells), 1)
+        low = jnp.logical_and(row == first, lane == 0)
+        high = jnp.logical_and(row == second, lane == cells - 1)
+        return jnp.logical_or(low, high).astype(jnp.float32)
+
+    for c in range(3):
+        planes = span_part(c)
+        plane_out[0, c] = planes[:, 0, :]
+        plane_out[1, c] = planes[:, planes.shape[1] - 1, :]
+        edge_out[c] = lax.dot_general(
+            hot(8, 0, 1),
+            stream_part(c).reshape(-1, cells),
+            (((1,), (1,)), ((), ())),
+            precision=HIGHEST,
+            preferred_element_type=jnp.float32,
+        )
+    pl.semaphore_wait(barrier, 4)
+    copies = []
+    for k, (source, target, device) in enumerate(
+        (
+            (edge_out, edge_in.at[0], right),
+            (edge_out, edge_in.at[1], left),
+            (plane_out.at[1], plane_in.at[0], after),
+            (plane_out.at[0], plane_in.at[1], before),
+        )
+    ):
+        copy = pltpu.make_async_remote_copy(
+            src_ref=source,
+            dst_ref=target,
+            send_sem=send_sem.at[k],
+            recv_sem=recv_sem.at[k],
+            device_id=device,
+            device_id_type=MESH,
+        )
+        copy.start()
+        copies.append(copy)
+    for copy in copies:
+        copy.wait()
+    for c in range(3):
+        spread[c] = lax.dot_general(
+            jnp.concatenate([edge_in[0, c], edge_in[1, c]]),
+            hot(16, 1, 8),
+            (((0,), (0,)), ((), ())),
+            precision=HIGHEST,
+            preferred_element_type=jnp.float32,
+        )
+
+
+def stream_difference(part, edges):
+    cells = part.shape[2]
+    lane = lax.broadcasted_iota(jnp.int32, part.shape, 2)
+    ahead = jnp.where(lane == cells - 1, edges, pltpu.roll(part, cells - 1, 2))
+    return ahead - jnp.where(lane == 0, edges, pltpu.roll(part, 1, 2))
+
+
+def span_difference(part, before, after):
+    planes = part.shape[1]
+    plane = lax.broadcasted_iota(jnp.int32, part.shape, 1)
+    ahead = jnp.where(plane == planes - 1, after[:, None, :], pltpu.roll(part, planes - 1, 1))
+    return ahead - jnp.where(plane == 0, before[:, None, :], pltpu.roll(part, 1, 1))
+
+
+def explicit_kernel(streams, spans, v_ref, explicit_ref, gs_ref, gp_ref, *refs):
+    exchange(streams, spans, lambda c: v_ref[c], lambda c: v_ref[c], refs)
+    plane_in, spread = refs[3], refs[4]
+    _, row_count, planes, cells = v_ref.shape
+
+    @pl.loop(0, row_count // 8)
+    def _(step):
+        base = pl.multiple_of(step * 8, 8)
+        rows = pl.ds(base, 8)
+        flat = pl.ds(pl.multiple_of(base * planes, 8), 8 * planes)
+        for c in range(3):
+            part = v_ref[c, rows]
+            gs = stream_difference(part, spread[c, flat].reshape(8, planes, cells))
+            gp = span_difference(part, plane_in[0, c, rows], plane_in[1, c, rows])
+            gs_ref[c, rows] = gs
+            gp_ref[c, rows] = gp
+            explicit_ref[c, rows] = part - ADVECT * (v_ref[0, rows] * gs + v_ref[2, rows] * gp)
+
+
+def adjoint_kernel(lines, streams, spans, v_ref, m_ref, gs_ref, gp_ref, wall_ref, out_ref, *refs):
+    exchange(
+        streams, spans, lambda c: v_ref[0] * m_ref[c], lambda c: v_ref[2] * m_ref[c], refs
+    )
+    plane_in, spread = refs[3], refs[4]
+    _, row_count, planes, cells = v_ref.shape
+
+    @pl.loop(0, row_count // 8)
+    def _(step):
+        base = pl.multiple_of(step * 8, 8)
+        rows = pl.ds(base, 8)
+        flat = pl.ds(pl.multiple_of(base * planes, 8), 8 * planes)
+        along, across = 0.0, 0.0
+        for c in range(3):
+            along = along + m_ref[c, rows] * gs_ref[c, rows]
+            across = across + m_ref[c, rows] * gp_ref[c, rows]
+        for c in range(3):
+            m = m_ref[c, rows]
+            edges = spread[c, flat].reshape(8, planes, cells)
+            diff = stream_difference(v_ref[0, rows] * m, edges) + span_difference(
+                v_ref[2, rows] * m, plane_in[0, c, rows], plane_in[1, c, rows]
+            )
+            if c == 0:
+                diff = diff - along
+            if c == 2:
+                diff = diff - across
+            out_ref[c, rows] = m + ADVECT * diff
+
+    line = lax.axis_index("line")
+
+    @pl.when(line == 0)
+    def _():
+        for c in range(3):
+            for k in range(WALL_ROWS):
+                out_ref[c, k] = out_ref[c, k] + wall_ref[c, k]
+
+    @pl.when(line == lines - 1)
+    def _():
+        for c in range(3):
+            for k in range(WALL_ROWS):
+                out_ref[c, row_count - 1 - k] = out_ref[c, row_count - 1 - k] + wall_ref[c, k]
+
+
+def halo_call(kernel, outs, collective_id, name, *args):
+    shape = args[0].shape
+    _, row_count, planes, cells = shape
+    vmem, dma = pltpu.VMEM, pltpu.SemaphoreType.DMA
+    full = jax.ShapeDtypeStruct(shape, jnp.float32)
+    return pl.pallas_call(
+        kernel,
+        out_shape=(full,) * outs,
+        in_specs=[VMEM] * len(args),
+        out_specs=(VMEM,) * outs,
+        scratch_shapes=[
+            vmem((3, 8, row_count * planes), jnp.float32),
+            vmem((2, 3, 8, row_count * planes), jnp.float32),
+            vmem((2, 3, row_count, cells), jnp.float32),
+            vmem((2, 3, row_count, cells), jnp.float32),
+            vmem((3, row_count * planes, cells), jnp.float32),
+            dma((4,)),
+            dma((4,)),
+        ],
+        compiler_params=pltpu.CompilerParams(
+            collective_id=collective_id, has_side_effects=True, vmem_limit_bytes=32 * 2**20
+        ),
+        name=name,
+    )(*args)
+
+
 def green_factors(diffusion):
     count = diffusion.shape[0]
     faces = jnp.concatenate([diffusion, diffusion[-1:]])
@@ -243,25 +407,6 @@
     return values[0], values[1, ::-1], 1.0 / totals[0, count - 1]
 
 
-def halos(shard, axis, dim):
-    peers, length = lax.axis_size(axis), shard.shape[dim]
-    last = lax.slice_in_dim(shard, length - 1, length, axis=dim)
-    first = lax.slice_in_dim(shard, 0, 1, axis=dim)
-    if peers == 2:
-        both = lax.ppermute(jnp.concatenate([first, last], axis=dim), axis, [(0, 1), (1, 0)])
-        return lax.slice_in_dim(both, 1, 2, axis=dim), lax.slice_in_dim(both, 0, 1, axis=dim)
-    up = [(i, (i + 1) % peers) for i in range(peers)]
-    return lax.ppermute(last, axis, up), lax.ppermute(first, axis, [(j, i) for i, j in up])
-
-
-def difference(shard, sides, dim):
-    before, after = sides
-    length = shard.shape[dim]
-    ahead = jnp.concatenate([lax.slice_in_dim(shard, 1, length, axis=dim), after], axis=dim)
-    behind = jnp.concatenate([before, lax.slice_in_dim(shard, 0, length - 1, axis=dim)], axis=dim)
-    return ahead - behind
-
-
 def local(velocity, cotangent, in_weight, in_bias, out_weight, diffusion, stencil, wall_mask):
     line_count = lax.axis_size("line")
     line_index = lax.axis_index("line")
@@ -292,9 +437,10 @@
     )
     operator = jnp.concatenate([green, low_own[None], high_own[None]])
 
-    grad_stream = difference(velocity, halos(velocity, "stream", 3), 3)
-    grad_span = difference(velocity, halos(velocity, "span", 2), 2)
-    explicit = velocity - ADVECT * (velocity[0] * grad_stream + velocity[2] * grad_span)
+    streams, spans = lax.axis_size("stream"), lax.axis_size("span")
+    explicit, grad_stream, grad_span = halo_call(
+        lambda *refs: explicit_kernel(streams, spans, *refs), 3, 3, "explicit", velocity
+    )
 
     weight_in = lax.dynamic_slice_in_dim(in_weight, line_index * share, share, 0)
     bias_in = lax.dynamic_slice_in_dim(in_bias, line_index * share, share, 0)
@@ -375,23 +521,17 @@
     totals, slab_grad = group_sum(packed, slab_part)
     extra_total = totals[share:].reshape(8, share)
     slab_grad = slab_grad.reshape(3, WALL_ROWS, planes, cells)
-
-    flux_stream = velocity[0] * multiplier
-    flux_span = velocity[2] * multiplier
-    stream_diff = difference(flux_stream, halos(flux_stream, "stream", 3), 3)
-    span_diff = difference(flux_span, halos(flux_span, "span", 2), 2)
-    adjoint = multiplier + ADVECT * (stream_diff + span_diff)
-    own = -ADVECT * jnp.stack(
-        [
-            jnp.sum(multiplier * grad_stream, axis=0),
-            jnp.zeros(multiplier.shape[1:], jnp.float32),
-            jnp.sum(multiplier * grad_span, axis=0),
-        ]
-    )
-    edge = jnp.where(at_top, slab_grad[:, ::-1], slab_grad)
-    rest = ((0, 0), (0, row_count - WALL_ROWS), (0, 0), (0, 0))
-    rest_top = ((0, 0), (row_count - WALL_ROWS, 0), (0, 0), (0, 0))
-    adjoint = adjoint + own + jnp.where(at_top, jnp.pad(edge, rest_top), jnp.pad(edge, rest))
+    (adjoint,) = halo_call(
+        lambda *refs: adjoint_kernel(line_count, streams, spans, *refs),
+        1,
+        4,
+        "adjoint",
+        velocity,
+        multiplier,
+        grad_stream,
+        grad_span,
+        slab_grad,
+    )
     return (
         new_velocity,
         adjoint,

time: 121 us -> 98.2 us (0.81)
  local copies, waits for them, and re-layouts: 44.2 us -> 17.5 us
  Pallas kernels: 33.2 us -> 52.4 us
  starting transfers between devices: 10.3 us -> 0 us
  matrix products: 14.6 us -> 11.5 us
    pallas_call x0 -> x2, Pallas kernels: none -> 18.5 us  [halo_call(): pl.pallas_call(kernel, out_shape=(full,) * outs, in_specs=[VMEM] * len(ar...]
    slice x12 -> x0, local copies, waits for them, and re-layouts: 12.4 us -> none  [the longest x4 3.25 us: halos(): first = lax.slice_in_dim(shard, 0, 1, axis=dim)]
    ppermute x6 -> x0, starting transfers between devices: 10.3 us -> none  [the longest x2 6.43 us: halos(): lax.ppermute(first, axis, [(j, i) for i, j in up])]
    unnamed x95 -> x36, local copies, waits for them, and re-layouts: 11.8 us -> 3.6 us
    ppermute x4 -> x0, local copies, waits for them, and re-layouts: 4.46 us -> none  [the longest x2 2.23 us: halos(): lax.ppermute(first, axis, [(j, i) for i, j in up])]
    sub x1 -> x0, other arithmetic: 3.36 us -> none  [local(): velocity - ADVECT * (velocity[0] * grad_stream + velocity[2] * grad_span)]
    mul x3 -> x0, local copies, waits for them, and re-layouts: 2.35 us -> none  [the longest x2 1.6 us: local(): velocity[0] * grad_stream + velocity[2] * grad_span]
    reduce_sum x1 -> x0, other arithmetic: 2.28 us -> none  [local(): jnp.sum(multiplier * grad_stream, axis=0)]
  transfers between devices with their start and end apart: 6 -> 0, of which waited for: 1 -> 0; matrix products, arithmetic and copies ran while one was open for 34% -> 0% of each run, Pallas kernels for 8% -> 0%
where the time goes in v3:
time: 98.2 us; the launch traced here: 97.2 us
  Pallas kernels  52.4 us (53%)
  local copies, waits for them, and re-layouts  17.5 us (18%)
  other arithmetic  12.8 us (13%)
  matrix products  11.5 us (12%)
  between operations  3 us (3%)
    pallas_call x2, Pallas kernels, halo_call(): pl.pallas_call(kernel, out_shape=(full,) * outs, in_specs=[VMEM] * len(ar...  18.5 us
    pallas_call x1, Pallas kernels, group_sum(): pl.pallas_call(lambda *refs: sum_kernel(lines, streams, spans, *refs), ou...  16 us
    pallas_call x2, Pallas kernels, line_gather(): pl.pallas_call(lambda *refs: gather_kernel(count, *refs), out_shape=jax.S...  16 us
    unnamed x36, local copies, waits for them, and re-layouts  3.6 us
    add x1, other arithmetic, local(): solved[3:, :row_count] + high_col * sum_below[3:, None]  2.64 us
    dot_general x1, matrix products, local(): lax.dot_general(stress_grad, hidden, contract, preferred_element_type=jnp...  2.23 us
    slice x2, local copies, waits for them, and re-layouts, green_factors(): return (values[0], values[1, ::-1], 1.0 / totals[0, count - 1])  2.04 us

profile of v3, /device:TPU:0, one launch (start us, length us, event | category | flops | bytes accessed | tf_op | source)
XLA Modules:
  0.0 97.2 jit_solution(1372512275127187790)
XLA Ops:
  2.5 1.3 %fusion.48 = (f32[1]{0:T(128)}, f32[1]{0:T(128)}) fusion(f32[256]{0:T(256)} %param.13), kind=kLoop, calls=%fused_computation.94 | loop fusion | bytes 16 | tf_op jit(solution)/shard_map/slice | solution.py:400
  3.8 1.4 %select_maximum_fusion.1 = (f32[8]{0:T(128)S(1)}, f32[8]{0:T(128)S(1)}) fusion(f32[1]{0:T(128)} %get-tuple-element.35, f32[1]{0:T(128)} %get-tuple-element.36), kind=kLoop, calls=%fused_computation.82 | loop fusion | flops 56 | bytes 72 | tf_op jit(solution)/shard_map/stack | solution.py:401
  5.2 1.3 %pad_maximum_fusion.5 = f32[257]{0:T(512)S(1)} fusion(f32[1]{0:T(128)} %get-tuple-element.36, f32[256]{0:T(256)} %param.13), kind=kLoop, calls=%fused_computation.71 | loop fusion | flops 257 | bytes 2056 | tf_op jit(solution)/shard_map/concatenate | solution.py:398
  10.1 1.9 %green.1 = (f32[8,256]{1,0:T(8,128)}, f32[8,256]{1,0:T(8,128)}) custom-call(f32[8,256]{1,0:T(8,128)} %pad.18.step_ref, f32[8,256]{1,0:T(8,128)} %pad.20.start_ref, f32[8,256]{1,0:T(8,128)} %pad.22.end_ref), custom_call_target="tpu_custom_call" | custom-call | tf_op jit(solution)/shard_map/green/pallas_call | solution.py:404
  11.9 1.3 %slice.130 = f32[1,1]{1,0:T(1,128)} slice(f32[8,256]{1,0:T(8,128)} %get-tuple-element.14), slice={[0:1], [255:256]} | slice | bytes 8 | tf_op jit(solution)/shard_map/slice | solution.py:407
  13.9 1.3 %fusion.46 = (f32[1,1]{1,0:T(1,128)}, f32[1,1]{1,0:T(1,128)}) fusion(f32[8,256]{1,0:T(8,128)} %get-tuple-element.13), kind=kLoop, calls=%fused_computation.92 | loop fusion | bytes 16 | tf_op jit(solution)/shard_map/slice | solution.py:476
  16.5 0.8 fusion.47
  18.6 0.8 iota_compare_fusion.1
  19.5 0.9 slice.134
  20.4 0.9 select_bitcast_fusion
  21.3 9.2 %line_gather.2 = f32[4,24,1024]{2,1,0:T(8,128)S(1)} custom-call(f32[24,1024]{1,0:T(8,128)S(1)} %bitcast.102), custom_call_target="tpu_custom_call" | custom-call | tf_op jit(solution)/shard_map/line_gather/pallas_call | solution.py:71
  32.1 1.3 %copy-done.4 = bf16[512,2048]{1,0:T(8,128)(2,1)} copy-done((bf16[512,2048]{1,0:T(8,128)(2,1)}, bf16[512,2048]{1,0:T(8,128)(2,1)S(1)}, u32[]{:S(2)}) %copy-start.4) | copy-done | bytes 2097176
  33.4 1.1 %fusion.31 = f32[3,2048]{1,0:T(4,128)S(1)} fusion(bf16[512,2048]{1,0:T(8,128)(2,1)S(1)} %tanh_convert_fusion, bf16[3,2048]{1,0:T(4,128)(2,1)} %param.12, s32[]{:T(128)S(6)} %select_n.23), kind=kOutput, calls=%fused_computation.69 | convolution fusion | flops 6291456 | bytes 2125828 | tf_op jit(solution)/shard_map/dot_general | solution.py:460
  35.2 8.7 %explicit.1 = (f32[3,64,8,128]{3,2,1,0:T(8,128)S(1)}, f32[3,64,8,128]{3,2,1,0:T(8,128)S(1)}, f32[3,64,8,128]{3,2,1,0:T(8,128)S(1)}) custom-call(f32[3,64,8,128]{3,2,1,0:T(8,128)S(1)} %copy-done.1), custom_call_target="tpu_custom_call" | custom-call | tf_op jit(solution)/shard_map/explicit/pallas_call | solution.py:375
  44.0 1.9 %fusion = f32[6,8,128,66]{2,3,1,0:T(8,128)S(1)} fusion(f32[6,64,8,128]{3,2,1,0:T(8,128)S(1)} %pad_maximum_fusion, f32[1,64]{0,1:T(8,128)S(1)} %copy.26, f32[1,64]{0,1:T(8,128)S(1)} %copy.25, f32[64,64]{0,1:T(8,128)S(1)} %select_multiply_fusion), kind=kOutput, calls=%fused_computation.4 | convolution fusion | flops 311435520 | bytes 3211776 | tf_op jit(solution)/shard_map/ij,cjzx->cizx/dot_general | solution.py:463
  46.3 1.1 %copy-done.6 = f32[6,8,128,66]{2,1,3,0:T(8,128)} copy-done((f32[6,8,128,66]{2,1,3,0:T(8,128)}, f32[6,8,128,66]{2,1,3,0:T(8,128)S(1)}, u32[]{:S(2)}) %copy-start.6) | copy-done | bytes 1622040
  47.5 6.7 %line_gather.3 = f32[4,24,1024]{2,1,0:T(8,128)S(1)} custom-call(f32[24,1024]{1,0:T(8,128)S(1)} %maximum_maximum_fusion.refs_0_), custom_call_target="tpu_custom_call" | custom-call | tf_op jit(solution)/shard_map/line_gather/pallas_call | solution.py:71
  55.7 2.2 %fusion.37 = f32[3,512]{1,0:T(4,128)S(1)} fusion(bf16[512,2048]{1,0:T(8,128)(2,1)} %copy-done.4, f32[1,3,16,128]{3,2,1,0:T(8,128)S(1)} %maximum_bitcast_fusion.2, f32[2048]{0:T(1024)S(1)} %get-tuple-element.29), kind=kOutput, calls=%fused_computation.84 | convolution fusion | flops 6303744 | bytes 2136064 | tf_op jit(solution)/shard_map/dot_general | solution.py:500
  57.9 1.6 %multiply_convert_fusion = bf16[512,2048]{1,0:T(8,128)(2,1)S(1)} fusion(bf16[512,2048]{1,0:T(8,128)(2,1)S(1)} %copy-done.5, bf16[3,2048]{1,0:T(4,128)(2,1)} %param.12, s32[]{:T(128)S(6)} %select_n.23, f32[1,3,16,128]{3,2,1,0:T(8,128)S(1)} %maximum_bitcast_fusion.2, f32[2048]{0:T(1024)S(1)} %get-tuple-element.29), kind=kOutput, calls=%fused_computation | convolution fusion | flops 11546624 | bytes 4231172 | tf_op jit(solution)/shard_map/dot_general | solution.py:493
  59.5 1.4 %fusion.6 = f32[512,128]{1,0:T(8,128)} fusion(bf16[512,2048]{1,0:T(8,128)(2,1)S(1)} %multiply_convert_fusion, bf16[128,1024]{1,0:T(8,128)(2,1)S(1)} %convolution_convert_fusion, bf16[128,1024]{1,0:T(8,128)(2,1)S(1)} %convolution_convert_fusion.1), kind=kOutput, calls=%fused_computation.17 | convolution fusion | flops 269484032 | bytes 2883584 | tf_op jit(solution)/shard_map/dot_general | solution.py:499
  65.2 2.6 %fusion.2 = (f32[3,64,8,128]{3,2,1,0:T(8,128)S(1)}, f32[3,64,8,128]{3,2,1,0:T(8,128)}) fusion(f32[6,66,8,128]{3,2,1,0:T(8,128)} %bitcast.105, f32[3,8,128]{2,1,0:T(8,128)S(1)} %get-tuple-element.28, f32[3,8,128]{2,1,0:T(8,128)S(1)} %get-tuple-element.25, f32[64]{0:T(128)} %copy-done.11, f32[64]{0:T(128)} %copy-done.10, ...), kind=kLoop, calls=%fused_computation.11 | loop fusion | flops 1572864 | bytes 3195392 | tf_op jit(solution)/shard_map/add | solution.py:481
  68.5 16.0 %group_sum.1 = (f32[576,128]{1,0:T(8,128)S(1)}, f32[24,1024]{1,0:T(8,128)S(1)}) custom-call(f32[576,128]{1,0:T(8,128)S(1)} %select_maximum_fusion.refs_0_, f32[2,24,1024]{2,1,0:T(8,128)S(1)} %pad_maximum_fusion.4.refs_1_), custom_call_target="tpu_custom_call" | custom-call | tf_op jit(solution)/shard_map/group_sum/pallas_call | solution.py:205
  84.6 9.8 %adjoint.1 = f32[3,64,8,128]{3,2,1,0:T(8,128)S(1)} custom-call(f32[3,64,8,128]{3,2,1,0:T(8,128)S(1)} %copy-done.1, f32[3,64,8,128]{3,2,1,0:T(8,128)S(1)} %get-tuple-element.19.refs_1_, f32[3,64,8,128]{3,2,1,0:T(8,128)S(1)} %get-tuple-element.15.refs_2_, f32[3,64,8,128]{3,2,1,0:T(8,128)S(1)} %copy-done.3, f32[3,8,8,128]{3,2,1,0:T(8,128)S(1)} %copy.66), custom_call_target="tpu_custom_call" | custom-call | tf_op jit(solution)/shard_map/adjoint/pallas_call | solution.py:375
  96.3 0.9 copy.70
  (87 shorter events, 17.7 us)
Async XLA Ops:
  0.6 30.7 %copy-start = (bf16[2048,128]{1,0:T(8,128)(2,1)S(1)}, bf16[2048,128]{1,0:T(8,128)(2,1)}, u32[]{:S(2)}) copy-start(bf16[2048,128]{1,0:T(8,128)(2,1)} %param.10) | copy-start | bytes 1572868
  17.5 13.1 %copy-start.10 = (f32[64]{0:T(128)}, f32[64]{0:T(128)S(1)}, u32[]{:S(2)}) copy-start(f32[64]{0:T(128)S(1)} %fusion.55) | copy-start | bytes 772
  17.6 13.0 %copy-start.11 = (f32[64]{0:T(128)}, f32[64]{0:T(128)S(1)}, u32[]{:S(2)}) copy-start(f32[64]{0:T(128)S(1)} %fusion.54) | copy-start | bytes 772
  31.3 3.9 %copy-start.1 = (f32[3,64,8,128]{3,2,1,0:T(8,128)S(1)}, f32[3,64,8,128]{3,2,1,0:T(8,128)}, u32[]{:S(2)}) copy-start(f32[3,64,8,128]{3,2,1,0:T(8,128)} %refs_0_.3) | copy-start | bytes 2359300
  32.1 1.3 %copy-start.4 = (bf16[512,2048]{1,0:T(8,128)(2,1)}, bf16[512,2048]{1,0:T(8,128)(2,1)S(1)}, u32[]{:S(2)}) copy-start(bf16[512,2048]{1,0:T(8,128)(2,1)S(1)} %tanh_convert_fusion) | copy-start | bytes 6291460
  33.4 10.5 %copy-start.7 = (f32[3,64,8,128]{3,2,1,0:T(8,128)S(1)}, f32[3,64,8,128]{3,2,1,0:T(8,128)}, u32[]{:S(2)}) copy-start(f32[3,64,8,128]{3,2,1,0:T(8,128)} %param.9) | copy-start | bytes 2359300
  43.9 2.0 %copy-start.2 = (f32[3,64,8,128]{3,2,1,0:T(8,128)}, f32[3,64,8,128]{3,2,1,0:T(8,128)S(1)}, u32[]{:S(2)}) copy-start(f32[3,64,8,128]{3,2,1,0:T(8,128)S(1)} %get-tuple-element.16.refs_3_) | copy-start | bytes 2359300
  45.9 1.5 %copy-start.9 = (f32[6,1024]{1,0:T(8,128)S(1)}, f32[6,1024]{1,0:T(8,128)}, u32[]{:S(2)}) copy-start(f32[6,1024]{1,0:T(8,128)} %reshape_reshape.3) | copy-start | bytes 73732
  45.9 1.5 %copy-start.13 = (f32[24]{0:T(128)S(1)}, f32[24]{0:T(128)}, u32[]{:S(2)}) copy-start(f32[24]{0:T(128)} %pad.35.clone) | copy-start | bytes 292
  46.2 1.2 %copy-start.6 = (f32[6,8,128,66]{2,1,3,0:T(8,128)}, f32[6,8,128,66]{2,1,3,0:T(8,128)S(1)}, u32[]{:S(2)}) copy-start(f32[6,8,128,66]{2,1,3,0:T(8,128)S(1)} %copy.65) | copy-start | bytes 4866052
  46.2 8.7 %copy-start.12 = (f32[4]{0:T(128)S(1)}, f32[4]{0:T(128)}, u32[]{:S(2)}) copy-start(f32[4]{0:T(128)} %get-tuple-element.40) | copy-start | bytes 52
  54.3 3.6 %copy-start.5 = (bf16[512,2048]{1,0:T(8,128)(2,1)S(1)}, bf16[512,2048]{1,0:T(8,128)(2,1)}, u32[]{:S(2)}) copy-start(bf16[512,2048]{1,0:T(8,128)(2,1)} %copy-done.4) | copy-start | bytes 6291460
  61.6 0.7 copy-start.14
  61.6 2.1 %copy-start.8 = (f32[512,128]{1,0:T(8,128)S(1)}, f32[512,128]{1,0:T(8,128)}, u32[]{:S(2)}) copy-start(f32[512,128]{1,0:T(8,128)} %fusion.6) | copy-start | bytes 786436
  65.2 19.4 %copy-start.3 = (f32[3,64,8,128]{3,2,1,0:T(8,128)S(1)}, f32[3,64,8,128]{3,2,1,0:T(8,128)}, u32[]{:S(2)}) copy-start(f32[3,64,8,128]{3,2,1,0:T(8,128)} %copy-done.2) | copy-start | bytes 2359300

commit v4 on v3

--- a/solution.py
+++ b/solution.py
@@ -10,28 +10,42 @@
 HIGHEST = lax.Precision.HIGHEST
 
 
-def prefix_kernel(step_ref, start_ref, end_ref, out_ref, total_ref):
-    step = step_ref[...]
-    count = step.shape[1]
-    lane = lax.broadcasted_iota(jnp.int32, step.shape, 1)
-    head = lane == 0
+def running_product(step, head, hop_of, keep_of):
     one = jnp.ones_like(step)
     zero = jnp.zeros_like(step)
     a, b = one, jnp.where(head, zero, step)
     c, d = jnp.where(head, zero, one), jnp.where(head, one, one + step)
     hop = 1
-    while hop < count:
-        keep = lane >= hop
-        pa = jnp.where(keep, pltpu.roll(a, hop, 1), one)
-        pb = jnp.where(keep, pltpu.roll(b, hop, 1), zero)
-        pc = jnp.where(keep, pltpu.roll(c, hop, 1), zero)
-        pd = jnp.where(keep, pltpu.roll(d, hop, 1), one)
+    while hop < step.shape[1]:
+        keep, turn = keep_of(hop), hop_of(hop)
+        pa = jnp.where(keep, pltpu.roll(a, turn, 1), one)
+        pb = jnp.where(keep, pltpu.roll(b, turn, 1), zero)
+        pc = jnp.where(keep, pltpu.roll(c, turn, 1), zero)
+        pd = jnp.where(keep, pltpu.roll(d, turn, 1), one)
         a, b, c, d = a * pa + b * pc, a * pb + b * pd, c * pa + d * pc, c * pb + d * pd
         hop *= 2
-    flux = start_ref[...] + 1.0
-    value = a + b * flux
-    out_ref[...] = value
-    total_ref[...] = c + d * flux + end_ref[...] * value
+    return a, b, c, d
+
+
+def factor_kernel(face_ref, low_ref, high_ref):
+    count = face_ref.shape[1]
+    face = jnp.broadcast_to(face_ref[...], (8, count))
+    lane = lax.broadcasted_iota(jnp.int32, face.shape, 1)
+    first, last = lane == 0, lane == count - 1
+
+    def only(where, value):
+        return jnp.sum(jnp.where(where, value, 0.0), axis=1, keepdims=True)
+
+    step = 1.0 / face
+    start, end = only(first, face), only(last, face)
+    a, b, c, d = running_product(step, first, lambda h: h, lambda h: lane >= h)
+    low = a + b * (start + 1.0)
+    wronskian = only(last, c + d * (start + 1.0) + end * low)
+    a, b, _, _ = running_product(
+        pltpu.roll(step, count - 1, 1), last, lambda h: count - h, lambda h: lane < count - h
+    )
+    low_ref[...] = low / wronskian
+    high_ref[...] = a + b * (end + 1.0)
 
 
 MESH = pl.DeviceIdType.MESH
@@ -395,16 +409,11 @@
 
 def green_factors(diffusion):
     count = diffusion.shape[0]
-    faces = jnp.concatenate([diffusion, diffusion[-1:]])
-    both = jnp.stack([faces[:-1], faces[:0:-1]])
-    starts = jnp.broadcast_to(jnp.stack([faces[0], faces[-1]])[:, None], (2, count))
-    ends = jnp.broadcast_to(jnp.stack([faces[-1], faces[0]])[:, None], (2, count))
-    pad = ((0, 6), (0, 0))
     shape = jax.ShapeDtypeStruct((8, count), jnp.float32)
-    values, totals = pl.pallas_call(prefix_kernel, out_shape=(shape, shape), name="green")(
-        jnp.pad(1.0 / both, pad), jnp.pad(starts, pad), jnp.pad(ends, pad)
-    )
-    return values[0], values[1, ::-1], 1.0 / totals[0, count - 1]
+    low, high = pl.pallas_call(factor_kernel, out_shape=(shape, shape), name="green")(
+        diffusion.reshape(1, count)
+    )
+    return low[0], high[0]
 
 
 def local(velocity, cotangent, in_weight, in_bias, out_weight, diffusion, stencil, wall_mask):
@@ -422,18 +431,15 @@
     slabs = line_gather(own_slab, 0)
     walls = (slabs[0], slabs[line_count - 1])
 
-    low, high, scale = green_factors(diffusion)
+    low, high = green_factors(diffusion)
     all_rows = low.shape[0]
     low_own = lax.dynamic_slice_in_dim(low, line_index * row_count, row_count)
     high_own = lax.dynamic_slice_in_dim(high, line_index * row_count, row_count)
     rows = jnp.arange(row_count)
-    green = (
-        jnp.where(
-            rows[:, None] >= rows[None, :],
-            high_own[:, None] * low_own[None, :],
-            low_own[:, None] * high_own[None, :],
-        )
-        * scale
+    green = jnp.where(
+        rows[:, None] >= rows[None, :],
+        high_own[:, None] * low_own[None, :],
+        low_own[:, None] * high_own[None, :],
     )
     operator = jnp.concatenate([green, low_own[None], high_own[None]])
 
@@ -469,12 +475,12 @@
     place = jnp.arange(line_count)
     below = (place < line_index).astype(jnp.float32)
     above = (place > line_index).astype(jnp.float32)
-    sum_below = jnp.sum(part[:, :, 0] * below[:, None, None, None], axis=0) * scale
-    sum_above = jnp.sum(part[:, :, 1] * above[:, None, None, None], axis=0) * scale
+    sum_below = jnp.sum(part[:, :, 0] * below[:, None, None, None], axis=0)
+    sum_above = jnp.sum(part[:, :, 1] * above[:, None, None, None], axis=0)
     mask_float = wall_mask.astype(jnp.float32)
     stress = jnp.sum(gathered[:, 12:18], axis=0).reshape(3, 2, planes, cells) * mask_float[None]
-    from_low = sum_below[:3] + stress[:, 0] * (low[0] * scale)
-    from_high = sum_above[:3] + stress[:, 1] * (high[all_rows - 1] * scale)
+    from_low = sum_below[:3] + stress[:, 0] * low[0]
+    from_high = sum_above[:3] + stress[:, 1] * high[all_rows - 1]
     low_col, high_col = low_own[None, :, None, None], high_own[None, :, None, None]
     new_velocity = solved[:3, :row_count] + high_col * from_low[:, None] + low_col * from_high[:, None]
     multiplier = (
@@ -484,8 +490,8 @@
     wall_total = jnp.sum(part[:, 3:], axis=0)
     wall_multiplier = jnp.stack(
         [
-            wall_total[:, 1] * (low[0] * scale),
-            wall_total[:, 0] * (high[all_rows - 1] * scale),
+            wall_total[:, 1] * low[0],
+            wall_total[:, 0] * high[all_rows - 1],
         ],
         axis=1,
     )

time: 98.2 us -> 91.9 us (0.936)
  local copies, waits for them, and re-layouts: 17.5 us -> 14.4 us
  between operations: 3 us -> 1.01 us
    pad x3 -> x0, local copies, waits for them, and re-layouts: 1.93 us -> none  [the longest x1 0.67 us: green_factors(): jnp.pad(starts, pad)]
    another operation x1 -> x0, other arithmetic: 1.37 us -> none  [green_factors(): jnp.stack([faces[-1], faces[0]])[:, None]]
    concatenate x1 -> x0, other arithmetic: 1.33 us -> none  [green_factors(): faces = jnp.concatenate([diffusion, diffusion[-1:]])]
    slice x1, other arithmetic: 0.77 us -> 2.07 us  [local(): sum_below[3:, None]]
    slice x6 -> x5, local copies, waits for them, and re-layouts: 4.74 us -> 4 us  [the longest x2 1.39 us: green_factors(): return (low[0], high[0])]
where the time goes in v4:
time: 91.9 us; the launch traced here: 91.2 us
  Pallas kernels  52.5 us (57%)
  local copies, waits for them, and re-layouts  14.4 us (16%)
  other arithmetic  11.9 us (13%)
  matrix products  11.5 us (13%)
  between operations  1.01 us (1%)
    pallas_call x2, Pallas kernels, halo_call(): pl.pallas_call(kernel, out_shape=(full,) * outs, in_specs=[VMEM] * len(ar...  18.5 us
    pallas_call x1, Pallas kernels, group_sum(): pl.pallas_call(lambda *refs: sum_kernel(lines, streams, spans, *refs), ou...  16 us
    pallas_call x2, Pallas kernels, line_gather(): pl.pallas_call(lambda *refs: gather_kernel(count, *refs), out_shape=jax.S...  16 us
    unnamed x36, local copies, waits for them, and re-layouts  3.6 us
    add x1, other arithmetic, local(): solved[3:, :row_count] + high_col * sum_below[3:, None]  2.64 us
    dot_general x1, matrix products, local(): lax.dot_general(stress_grad, hidden, contract, preferred_element_type=jnp...  2.23 us
    slice x1, other arithmetic, local(): sum_below[3:, None]  2.07 us
    pallas_call x1, Pallas kernels, green_factors(): pl.pallas_call(factor_kernel, out_shape=(shape, shape), name='green')  1.95 us

profile of v4, /device:TPU:0, one launch (start us, length us, event | category | flops | bytes accessed | tf_op | source)
XLA Modules:
  0.0 91.2 jit_solution(3271659689685027014)
XLA Ops:
  2.4 0.8 dynamic_slice.19
  3.2 1.9 %green.1 = (f32[8,256]{1,0:T(8,128)}, f32[8,256]{1,0:T(8,128)}) custom-call(f32[1,256]{1,0:T(1,128)} %bitcast.101), custom_call_target="tpu_custom_call" | custom-call | tf_op jit(solution)/shard_map/green/pallas_call | solution.py:413
  5.1 1.3 %slice.126 = f32[1,1]{1,0:T(1,128)} slice(f32[8,256]{1,0:T(8,128)} %get-tuple-element.14), slice={[0:1], [0:1]} | slice | bytes 8 | tf_op jit(solution)/shard_map/slice | solution.py:482
  6.4 1.3 %slice.130 = f32[1,1]{1,0:T(1,128)} slice(f32[8,256]{1,0:T(8,128)} %get-tuple-element.13), slice={[0:1], [255:256]} | slice | bytes 8 | tf_op jit(solution)/shard_map/slice | solution.py:483
  9.9 0.8 iota_compare_fusion.1
  11.0 0.9 slice.116
  11.9 0.9 select_bitcast_fusion
  12.8 9.2 %line_gather.2 = f32[4,24,1024]{2,1,0:T(8,128)S(1)} custom-call(f32[24,1024]{1,0:T(8,128)S(1)} %bitcast.88), custom_call_target="tpu_custom_call" | custom-call | tf_op jit(solution)/shard_map/line_gather/pallas_call | solution.py:85
  23.5 1.3 %copy-done.4 = bf16[512,2048]{1,0:T(8,128)(2,1)} copy-done((bf16[512,2048]{1,0:T(8,128)(2,1)}, bf16[512,2048]{1,0:T(8,128)(2,1)S(1)}, u32[]{:S(2)}) %copy-start.4) | copy-done | bytes 2097176
  24.9 1.1 %fusion.30 = f32[3,2048]{1,0:T(4,128)S(1)} fusion(bf16[512,2048]{1,0:T(8,128)(2,1)S(1)} %tanh_convert_fusion, bf16[3,2048]{1,0:T(4,128)(2,1)} %param.12, s32[]{:T(128)S(6)} %select_n.23), kind=kOutput, calls=%fused_computation.66 | convolution fusion | flops 6291456 | bytes 2125828 | tf_op jit(solution)/shard_map/dot_general | solution.py:466
  26.6 8.7 %explicit.1 = (f32[3,64,8,128]{3,2,1,0:T(8,128)S(1)}, f32[3,64,8,128]{3,2,1,0:T(8,128)S(1)}, f32[3,64,8,128]{3,2,1,0:T(8,128)S(1)}) custom-call(f32[3,64,8,128]{3,2,1,0:T(8,128)S(1)} %copy-done.1), custom_call_target="tpu_custom_call" | custom-call | tf_op jit(solution)/shard_map/explicit/pallas_call | solution.py:389
  35.5 1.9 %fusion = f32[6,8,128,66]{2,3,1,0:T(8,128)S(1)} fusion(f32[6,64,8,128]{3,2,1,0:T(8,128)S(1)} %pad_maximum_fusion, f32[1,64]{0,1:T(8,128)S(1)} %copy.18, f32[1,64]{0,1:T(8,128)S(1)} %copy.17, f32[64,64]{0,1:T(8,128)S(1)} %multiply_select_fusion), kind=kOutput, calls=%fused_computation.4 | convolution fusion | flops 311435520 | bytes 3211776 | tf_op jit(solution)/shard_map/ij,cjzx->cizx/dot_general | solution.py:469
  37.7 1.1 %copy-done.6 = f32[6,8,128,66]{2,1,3,0:T(8,128)} copy-done((f32[6,8,128,66]{2,1,3,0:T(8,128)}, f32[6,8,128,66]{2,1,3,0:T(8,128)S(1)}, u32[]{:S(2)}) %copy-start.6) | copy-done | bytes 1622040
  38.9 6.7 %line_gather.3 = f32[4,24,1024]{2,1,0:T(8,128)S(1)} custom-call(f32[24,1024]{1,0:T(8,128)S(1)} %maximum_maximum_fusion.refs_0_), custom_call_target="tpu_custom_call" | custom-call | tf_op jit(solution)/shard_map/line_gather/pallas_call | solution.py:85
  47.1 1.3 %slice_multiply_fusion.1 = (f32[3,1,8,128]{3,2,1,0:T(8,128)S(1)}, f32[3,1,8,128]{3,2,1,0:T(8,128)S(1)}) fusion(f32[3,2,8,128]{3,2,1,0:T(8,128)S(1)} %slice_reduce_fusion.1, f32[]{:T(128)} %bitcast.11, f32[]{:T(128)} %bitcast.14), kind=kLoop, calls=%fused_computation.55 | loop fusion | flops 6144 | bytes 49160 | tf_op jit(solution)/shard_map/mul | solution.py:493
  48.5 2.2 %fusion.36 = f32[3,512]{1,0:T(4,128)S(1)} fusion(bf16[512,2048]{1,0:T(8,128)(2,1)} %copy-done.4, f32[1,3,16,128]{3,2,1,0:T(8,128)S(1)} %maximum_bitcast_fusion.2, f32[2048]{0:T(1024)S(1)} %get-tuple-element.29), kind=kOutput, calls=%fused_computation.77 | convolution fusion | flops 6303744 | bytes 2136064 | tf_op jit(solution)/shard_map/dot_general | solution.py:506
  50.7 1.6 %multiply_convert_fusion = bf16[512,2048]{1,0:T(8,128)(2,1)S(1)} fusion(bf16[512,2048]{1,0:T(8,128)(2,1)S(1)} %copy-done.5, bf16[3,2048]{1,0:T(4,128)(2,1)} %param.12, s32[]{:T(128)S(6)} %select_n.23, f32[1,3,16,128]{3,2,1,0:T(8,128)S(1)} %maximum_bitcast_fusion.2, f32[2048]{0:T(1024)S(1)} %get-tuple-element.29), kind=kOutput, calls=%fused_computation | convolution fusion | flops 11546624 | bytes 4231172 | tf_op jit(solution)/shard_map/dot_general | solution.py:499
  52.3 1.4 %fusion.6 = f32[512,128]{1,0:T(8,128)} fusion(bf16[512,2048]{1,0:T(8,128)(2,1)S(1)} %multiply_convert_fusion, bf16[128,1024]{1,0:T(8,128)(2,1)S(1)} %convolution_convert_fusion, bf16[128,1024]{1,0:T(8,128)(2,1)S(1)} %convolution_convert_fusion.1), kind=kOutput, calls=%fused_computation.17 | convolution fusion | flops 269484032 | bytes 2883584 | tf_op jit(solution)/shard_map/dot_general | solution.py:505
  57.1 2.1 %fusion.44 = (f32[3,8,128]{2,1,0:T(8,128)S(1)}, f32[3,8,128]{2,1,0:T(8,128)S(1)}, f32[3,8,128]{2,1,0:T(8,128)S(1)}, f32[3,8,128]{2,1,0:T(8,128)S(1)}) fusion(f32[6,8,128]{2,1,0:T(8,128)} %fusion.13, f32[]{:T(128)} %bitcast.11, f32[3,2,8,128]{3,2,1,0:T(8,128)} %broadcast_multiply_fusion, f32[]{:T(128)} %bitcast.14, f32[6,8,128]{2,1,0:T(8,128)S(1)} %fusion.11), kind=kLoop, calls=%fused_computation.84 | loop fusion | flops 12288 | bytes 122888 | tf_op jit(solution)/shard_map/slice | solution.py:487
  59.2 2.6 %fusion.2 = (f32[3,64,8,128]{3,2,1,0:T(8,128)S(1)}, f32[3,64,8,128]{3,2,1,0:T(8,128)}) fusion(f32[6,66,8,128]{3,2,1,0:T(8,128)} %bitcast.91, f32[3,8,128]{2,1,0:T(8,128)S(1)} %get-tuple-element.28, f32[3,8,128]{2,1,0:T(8,128)S(1)} %get-tuple-element.25, f32[64]{0:T(128)} %bitcast.98, f32[64]{0:T(128)} %bitcast.100, f32[3,8,128]{2,1,0:T(8,128)S(1)} %get-tuple-element.27, ...), kind=kLoop, calls=%fused_computation.11 | loop fusion | flops 1572864 | bytes 3195392 | tf_op jit(solution)/shard_map/add | solution.py:487
  62.5 16.0 %group_sum.1 = (f32[576,128]{1,0:T(8,128)S(1)}, f32[24,1024]{1,0:T(8,128)S(1)}) custom-call(f32[576,128]{1,0:T(8,128)S(1)} %select_maximum_fusion.refs_0_, f32[2,24,1024]{2,1,0:T(8,128)S(1)} %pad_maximum_fusion.4.refs_1_), custom_call_target="tpu_custom_call" | custom-call | tf_op jit(solution)/shard_map/group_sum/pallas_call | solution.py:219
  78.6 9.8 %adjoint.1 = f32[3,64,8,128]{3,2,1,0:T(8,128)S(1)} custom-call(f32[3,64,8,128]{3,2,1,0:T(8,128)S(1)} %copy-done.1, f32[3,64,8,128]{3,2,1,0:T(8,128)S(1)} %get-tuple-element.19.refs_1_, f32[3,64,8,128]{3,2,1,0:T(8,128)S(1)} %get-tuple-element.15.refs_2_, f32[3,64,8,128]{3,2,1,0:T(8,128)S(1)} %copy-done.3, f32[3,8,8,128]{3,2,1,0:T(8,128)S(1)} %copy.54), custom_call_target="tpu_custom_call" | custom-call | tf_op jit(solution)/shard_map/adjoint/pallas_call | solution.py:389
  89.0 0.7 slice.139
  90.3 0.9 copy.58
  (73 shorter events, 13.5 us)
Async XLA Ops:
  0.6 22.2 %copy-start = (bf16[2048,128]{1,0:T(8,128)(2,1)S(1)}, bf16[2048,128]{1,0:T(8,128)(2,1)}, u32[]{:S(2)}) copy-start(bf16[2048,128]{1,0:T(8,128)(2,1)} %param.10) | copy-start | bytes 1572868
  9.2 1.6 %copy-start.10 = (f32[1,64]{1,0:T(1,128)}, f32[1,64]{1,0:T(1,128)S(1)}, u32[]{:S(2)}) copy-start(f32[1,64]{1,0:T(1,128)S(1)} %get-tuple-element.33) | copy-start | bytes 772
  9.2 12.9 %copy-start.11 = (f32[1,64]{1,0:T(1,128)}, f32[1,64]{1,0:T(1,128)S(1)}, u32[]{:S(2)}) copy-start(f32[1,64]{1,0:T(1,128)S(1)} %get-tuple-element.34) | copy-start | bytes 772
  22.8 3.8 %copy-start.1 = (f32[3,64,8,128]{3,2,1,0:T(8,128)S(1)}, f32[3,64,8,128]{3,2,1,0:T(8,128)}, u32[]{:S(2)}) copy-start(f32[3,64,8,128]{3,2,1,0:T(8,128)} %refs_0_.3) | copy-start | bytes 2359300
  23.5 1.3 %copy-start.4 = (bf16[512,2048]{1,0:T(8,128)(2,1)}, bf16[512,2048]{1,0:T(8,128)(2,1)S(1)}, u32[]{:S(2)}) copy-start(bf16[512,2048]{1,0:T(8,128)(2,1)S(1)} %tanh_convert_fusion) | copy-start | bytes 6291460
  24.9 10.5 %copy-start.7 = (f32[3,64,8,128]{3,2,1,0:T(8,128)S(1)}, f32[3,64,8,128]{3,2,1,0:T(8,128)}, u32[]{:S(2)}) copy-start(f32[3,64,8,128]{3,2,1,0:T(8,128)} %param.9) | copy-start | bytes 2359300
  35.3 2.0 %copy-start.2 = (f32[3,64,8,128]{3,2,1,0:T(8,128)}, f32[3,64,8,128]{3,2,1,0:T(8,128)S(1)}, u32[]{:S(2)}) copy-start(f32[3,64,8,128]{3,2,1,0:T(8,128)S(1)} %get-tuple-element.16.refs_3_) | copy-start | bytes 2359300
  37.4 1.5 %copy-start.9 = (f32[6,1024]{1,0:T(8,128)S(1)}, f32[6,1024]{1,0:T(8,128)}, u32[]{:S(2)}) copy-start(f32[6,1024]{1,0:T(8,128)} %reshape_reshape.3) | copy-start | bytes 73732
  37.4 1.5 %copy-start.13 = (f32[24]{0:T(128)S(1)}, f32[24]{0:T(128)}, u32[]{:S(2)}) copy-start(f32[24]{0:T(128)} %pad.16.clone) | copy-start | bytes 292
  37.7 1.2 %copy-start.6 = (f32[6,8,128,66]{2,1,3,0:T(8,128)}, f32[6,8,128,66]{2,1,3,0:T(8,128)S(1)}, u32[]{:S(2)}) copy-start(f32[6,8,128,66]{2,1,3,0:T(8,128)S(1)} %copy.53) | copy-start | bytes 4866052
  37.7 8.8 %copy-start.12 = (f32[4]{0:T(128)S(1)}, f32[4]{0:T(128)}, u32[]{:S(2)}) copy-start(f32[4]{0:T(128)} %get-tuple-element.32) | copy-start | bytes 52
  45.8 4.9 %copy-start.5 = (bf16[512,2048]{1,0:T(8,128)(2,1)S(1)}, bf16[512,2048]{1,0:T(8,128)(2,1)}, u32[]{:S(2)}) copy-start(bf16[512,2048]{1,0:T(8,128)(2,1)} %copy-done.4) | copy-start | bytes 6291460
  54.4 0.7 copy-start.14
  54.4 2.1 %copy-start.8 = (f32[512,128]{1,0:T(8,128)S(1)}, f32[512,128]{1,0:T(8,128)}, u32[]{:S(2)}) copy-start(f32[512,128]{1,0:T(8,128)} %fusion.6) | copy-start | bytes 786436
  59.2 19.4 %copy-start.3 = (f32[3,64,8,128]{3,2,1,0:T(8,128)S(1)}, f32[3,64,8,128]{3,2,1,0:T(8,128)}, u32[]{:S(2)}) copy-start(f32[3,64,8,128]{3,2,1,0:T(8,128)} %copy-done.2) | copy-start | bytes 2359300

commit v5 on v4

--- a/solution.py
+++ b/solution.py
@@ -262,27 +262,7 @@
         high = jnp.logical_and(row == second, lane == cells - 1)
         return jnp.logical_or(low, high).astype(jnp.float32)
 
-    for c in range(3):
-        planes = span_part(c)
-        plane_out[0, c] = planes[:, 0, :]
-        plane_out[1, c] = planes[:, planes.shape[1] - 1, :]
-        edge_out[c] = lax.dot_general(
-            hot(8, 0, 1),
-            stream_part(c).reshape(-1, cells),
-            (((1,), (1,)), ((), ())),
-            precision=HIGHEST,
-            preferred_element_type=jnp.float32,
-        )
-    pl.semaphore_wait(barrier, 4)
-    copies = []
-    for k, (source, target, device) in enumerate(
-        (
-            (edge_out, edge_in.at[0], right),
-            (edge_out, edge_in.at[1], left),
-            (plane_out.at[1], plane_in.at[0], after),
-            (plane_out.at[0], plane_in.at[1], before),
-        )
-    ):
+    def send(k, source, target, device):
         copy = pltpu.make_async_remote_copy(
             src_ref=source,
             dst_ref=target,
@@ -292,7 +272,26 @@
             device_id_type=MESH,
         )
         copy.start()
-        copies.append(copy)
+        return copy
+
+    for c in range(3):
+        planes = span_part(c)
+        plane_out[0, c] = planes[:, 0, :]
+        plane_out[1, c] = planes[:, planes.shape[1] - 1, :]
+    pl.semaphore_wait(barrier, 4)
+    copies = [
+        send(0, plane_out.at[1], plane_in.at[0], after),
+        send(1, plane_out.at[0], plane_in.at[1], before),
+    ]
+    for c in range(3):
+        edge_out[c] = lax.dot_general(
+            hot(8, 0, 1),
+            stream_part(c).reshape(-1, cells),
+            (((1,), (1,)), ((), ())),
+            precision=HIGHEST,
+            preferred_element_type=jnp.float32,
+        )
+    copies += [send(2, edge_out, edge_in.at[0], right), send(3, edge_out, edge_in.at[1], left)]
     for copy in copies:
         copy.wait()
     for c in range(3):
@@ -432,7 +431,6 @@
     walls = (slabs[0], slabs[line_count - 1])
 
     low, high = green_factors(diffusion)
-    all_rows = low.shape[0]
     low_own = lax.dynamic_slice_in_dim(low, line_index * row_count, row_count)
     high_own = lax.dynamic_slice_in_dim(high, line_index * row_count, row_count)
     rows = jnp.arange(row_count)
@@ -480,7 +478,7 @@
     mask_float = wall_mask.astype(jnp.float32)
     stress = jnp.sum(gathered[:, 12:18], axis=0).reshape(3, 2, planes, cells) * mask_float[None]
     from_low = sum_below[:3] + stress[:, 0] * low[0]
-    from_high = sum_above[:3] + stress[:, 1] * high[all_rows - 1]
+    from_high = sum_above[:3] + stress[:, 1]
     low_col, high_col = low_own[None, :, None, None], high_own[None, :, None, None]
     new_velocity = solved[:3, :row_count] + high_col * from_low[:, None] + low_col * from_high[:, None]
     multiplier = (
@@ -491,7 +489,7 @@
     wall_multiplier = jnp.stack(
         [
             wall_total[:, 1] * low[0],
-            wall_total[:, 0] * high[all_rows - 1],
+            wall_total[:, 0],
         ],
         axis=1,
     )

time: 91.9 us -> 90.3 us (0.983)
  other arithmetic: 11.9 us -> 10.5 us
  local copies, waits for them, and re-layouts: 14.4 us -> 13 us
  Pallas kernels: 52.5 us -> 53.6 us
    slice x1 -> x0, local copies, waits for them, and re-layouts: 1.34 us -> none  [local(): from_high = sum_above[:3] + stress[:, 1] * high[all_rows - 1]]
where the time goes in v5:
time: 90.3 us; the launch traced here: 89.6 us
  Pallas kernels  53.6 us (59%)
  local copies, waits for them, and re-layouts  13 us (14%)
  matrix products  11.4 us (13%)
  other arithmetic  10.5 us (12%)
  between operations  1.01 us (1%)
    pallas_call x2, Pallas kernels, halo_call(): pl.pallas_call(kernel, out_shape=(full,) * outs, in_specs=[VMEM] * len(ar...  19.4 us
    pallas_call x1, Pallas kernels, group_sum(): pl.pallas_call(lambda *refs: sum_kernel(lines, streams, spans, *refs), ou...  16.3 us
    pallas_call x2, Pallas kernels, line_gather(): pl.pallas_call(lambda *refs: gather_kernel(count, *refs), out_shape=jax.S...  16 us
    unnamed x36, local copies, waits for them, and re-layouts  3.62 us
    add x1, other arithmetic, local(): solved[3:, :row_count] + high_col * sum_below[3:, None]  2.64 us
    dot_general x1, matrix products, local(): lax.dot_general(stress_grad, hidden, contract, preferred_element_type=jnp...  2.23 us
    pallas_call x1, Pallas kernels, green_factors(): pl.pallas_call(factor_kernel, out_shape=(shape, shape), name='green')  1.95 us
    dot_general x1, matrix products, local(): solved = jnp.einsum('ij,cjzx->cizx', operator, both, precision=HIGHEST)  1.88 us

profile of v5, /device:TPU:0, one launch (start us, length us, event | category | flops | bytes accessed | tf_op | source)
XLA Modules:
  0.0 89.6 jit_solution(8381841719971371529)
XLA Ops:
  2.4 0.8 dynamic_slice.19
  3.2 1.9 %green.1 = (f32[8,256]{1,0:T(8,128)}, f32[8,256]{1,0:T(8,128)}) custom-call(f32[1,256]{1,0:T(1,128)} %bitcast.100), custom_call_target="tpu_custom_call" | custom-call | tf_op jit(solution)/shard_map/green/pallas_call | solution.py:412
  5.1 1.3 %slice.120 = f32[1,1]{1,0:T(1,128)} slice(f32[8,256]{1,0:T(8,128)} %get-tuple-element.14), slice={[0:1], [0:1]} | slice | bytes 8 | tf_op jit(solution)/shard_map/slice | solution.py:480
  8.6 0.8 iota_compare_fusion.1
  9.6 0.9 %slice.110 = f32[3,8,8,128]{3,2,1,0:T(8,128)S(1)} slice(f32[3,64,8,128]{3,2,1,0:T(8,128)} %refs_0_.3), slice={[0:3], [56:64], [0:8], [0:128]} | slice | bytes 196608 | tf_op jit(solution)/shard_map/slice | solution.py:428
  10.5 0.9 %select_bitcast_fusion = f32[3,8,8,128]{3,2,1,0:T(8,128)S(1)} fusion(f32[3,64,8,128]{3,2,1,0:T(8,128)} %refs_0_.3, f32[3,8,8,128]{3,2,1,0:T(8,128)S(1)} %slice.110, pred[]{:T(512)S(6)} %eq.19), kind=kLoop, calls=%fused_computation.40 | loop fusion | flops 24576 | bytes 294913
  11.5 9.2 %line_gather.2 = f32[4,24,1024]{2,1,0:T(8,128)S(1)} custom-call(f32[24,1024]{1,0:T(8,128)S(1)} %bitcast.87), custom_call_target="tpu_custom_call" | custom-call | tf_op jit(solution)/shard_map/line_gather/pallas_call | solution.py:85
  21.5 0.7 tanh_convert_fusion
  22.2 1.3 %copy-done.4 = bf16[512,2048]{1,0:T(8,128)(2,1)} copy-done((bf16[512,2048]{1,0:T(8,128)(2,1)}, bf16[512,2048]{1,0:T(8,128)(2,1)S(1)}, u32[]{:S(2)}) %copy-start.4) | copy-done | bytes 2097176
  23.5 1.1 %fusion.29 = f32[3,2048]{1,0:T(4,128)S(1)} fusion(bf16[512,2048]{1,0:T(8,128)(2,1)S(1)} %tanh_convert_fusion, bf16[3,2048]{1,0:T(4,128)(2,1)} %param.12, s32[]{:T(128)S(6)} %select_n.23), kind=kOutput, calls=%fused_computation.64 | convolution fusion | flops 6291456 | bytes 2125828 | tf_op jit(solution)/shard_map/dot_general | solution.py:464
  25.3 9.2 %explicit.1 = (f32[3,64,8,128]{3,2,1,0:T(8,128)S(1)}, f32[3,64,8,128]{3,2,1,0:T(8,128)S(1)}, f32[3,64,8,128]{3,2,1,0:T(8,128)S(1)}) custom-call(f32[3,64,8,128]{3,2,1,0:T(8,128)S(1)} %copy-done.1), custom_call_target="tpu_custom_call" | custom-call | tf_op jit(solution)/shard_map/explicit/pallas_call | solution.py:388
  34.6 1.9 %fusion = f32[6,8,128,66]{2,3,1,0:T(8,128)S(1)} fusion(f32[6,64,8,128]{3,2,1,0:T(8,128)S(1)} %pad_maximum_fusion, f32[1,64]{0,1:T(8,128)S(1)} %copy.18, f32[1,64]{0,1:T(8,128)S(1)} %copy.17, f32[64,64]{0,1:T(8,128)S(1)} %multiply_select_fusion), kind=kOutput, calls=%fused_computation.4 | convolution fusion | flops 311435520 | bytes 3211776 | tf_op jit(solution)/shard_map/ij,cjzx->cizx/dot_general | solution.py:467
  36.9 1.1 %copy-done.6 = f32[6,8,128,66]{2,1,3,0:T(8,128)} copy-done((f32[6,8,128,66]{2,1,3,0:T(8,128)}, f32[6,8,128,66]{2,1,3,0:T(8,128)S(1)}, u32[]{:S(2)}) %copy-start.6) | copy-done | bytes 1622040
  38.1 6.8 %line_gather.3 = f32[4,24,1024]{2,1,0:T(8,128)S(1)} custom-call(f32[24,1024]{1,0:T(8,128)S(1)} %maximum_maximum_fusion.refs_0_), custom_call_target="tpu_custom_call" | custom-call | tf_op jit(solution)/shard_map/line_gather/pallas_call | solution.py:85
  47.0 2.2 %fusion.35 = f32[3,512]{1,0:T(4,128)S(1)} fusion(bf16[512,2048]{1,0:T(8,128)(2,1)} %copy-done.4, f32[1,3,16,128]{3,2,1,0:T(8,128)S(1)} %maximum_bitcast_fusion.2, f32[2048]{0:T(1024)S(1)} %get-tuple-element.29), kind=kOutput, calls=%fused_computation.75 | convolution fusion | flops 6303744 | bytes 2136064 | tf_op jit(solution)/shard_map/dot_general | solution.py:504
  49.2 1.6 %multiply_convert_fusion = bf16[512,2048]{1,0:T(8,128)(2,1)S(1)} fusion(bf16[512,2048]{1,0:T(8,128)(2,1)S(1)} %copy-done.5, bf16[3,2048]{1,0:T(4,128)(2,1)} %param.12, s32[]{:T(128)S(6)} %select_n.23, f32[1,3,16,128]{3,2,1,0:T(8,128)S(1)} %maximum_bitcast_fusion.2, f32[2048]{0:T(1024)S(1)} %get-tuple-element.29), kind=kOutput, calls=%fused_computation | convolution fusion | flops 11546624 | bytes 4231172 | tf_op jit(solution)/shard_map/dot_general | solution.py:497
  50.8 1.4 %fusion.6 = f32[512,128]{1,0:T(8,128)} fusion(bf16[512,2048]{1,0:T(8,128)(2,1)S(1)} %multiply_convert_fusion, bf16[128,1024]{1,0:T(8,128)(2,1)S(1)} %convolution_convert_fusion, bf16[128,1024]{1,0:T(8,128)(2,1)S(1)} %convolution_convert_fusion.1), kind=kOutput, calls=%fused_computation.17 | convolution fusion | flops 269484032 | bytes 2883584 | tf_op jit(solution)/shard_map/dot_general | solution.py:503
  54.3 0.7 reshape.78
  55.7 1.4 %fusion.43 = (f32[3,8,128]{2,1,0:T(8,128)S(1)}, f32[3,8,128]{2,1,0:T(8,128)S(1)}, f32[3,8,128]{2,1,0:T(8,128)S(1)}, f32[3,8,128]{2,1,0:T(8,128)S(1)}) fusion(f32[6,8,128]{2,1,0:T(8,128)} %fusion.13, f32[]{:T(128)} %bitcast.11, f32[3,2,8,128]{3,2,1,0:T(8,128)} %broadcast_multiply_fusion, f32[6,8,128]{2,1,0:T(8,128)S(1)} %fusion.11), kind=kLoop, calls=%fused_computation.82 | loop fusion | flops 9216 | bytes 122884 | tf_op jit(solution)/shard_map/slice | solution.py:485
  57.1 2.6 %fusion.2 = (f32[3,64,8,128]{3,2,1,0:T(8,128)S(1)}, f32[3,64,8,128]{3,2,1,0:T(8,128)}) fusion(f32[6,66,8,128]{3,2,1,0:T(8,128)} %bitcast.90, f32[3,8,128]{2,1,0:T(8,128)S(1)} %get-tuple-element.28, f32[3,8,128]{2,1,0:T(8,128)S(1)} %get-tuple-element.25, f32[64]{0:T(128)} %bitcast.97, f32[64]{0:T(128)} %bitcast.99, f32[3,8,128]{2,1,0:T(8,128)S(1)} %get-tuple-element.27, ...), kind=kLoop, calls=%fused_computation.11 | loop fusion | flops 1572864 | bytes 3195392 | tf_op jit(solution)/shard_map/add | solution.py:485
  60.3 16.3 %group_sum.1 = (f32[576,128]{1,0:T(8,128)S(1)}, f32[24,1024]{1,0:T(8,128)S(1)}) custom-call(f32[576,128]{1,0:T(8,128)S(1)} %select_maximum_fusion.refs_0_, f32[2,24,1024]{2,1,0:T(8,128)S(1)} %pad_maximum_fusion.4.refs_1_), custom_call_target="tpu_custom_call" | custom-call | tf_op jit(solution)/shard_map/group_sum/pallas_call | solution.py:219
  76.6 10.2 %adjoint.1 = f32[3,64,8,128]{3,2,1,0:T(8,128)S(1)} custom-call(f32[3,64,8,128]{3,2,1,0:T(8,128)S(1)} %copy-done.1, f32[3,64,8,128]{3,2,1,0:T(8,128)S(1)} %get-tuple-element.19.refs_1_, f32[3,64,8,128]{3,2,1,0:T(8,128)S(1)} %get-tuple-element.15.refs_2_, f32[3,64,8,128]{3,2,1,0:T(8,128)S(1)} %copy-done.3, f32[3,8,8,128]{3,2,1,0:T(8,128)S(1)} %copy.54), custom_call_target="tpu_custom_call" | custom-call | tf_op jit(solution)/shard_map/adjoint/pallas_call | solution.py:388
  87.4 0.7 slice.132
  88.7 0.9 copy.58
  (72 shorter events, 12.7 us)
Async XLA Ops:
  0.6 20.8 %copy-start = (bf16[2048,128]{1,0:T(8,128)(2,1)S(1)}, bf16[2048,128]{1,0:T(8,128)(2,1)}, u32[]{:S(2)}) copy-start(bf16[2048,128]{1,0:T(8,128)(2,1)} %param.10) | copy-start | bytes 1572868
  7.9 1.6 %copy-start.10 = (f32[1,64]{1,0:T(1,128)}, f32[1,64]{1,0:T(1,128)S(1)}, u32[]{:S(2)}) copy-start(f32[1,64]{1,0:T(1,128)S(1)} %get-tuple-element.33) | copy-start | bytes 772
  7.9 12.9 %copy-start.11 = (f32[1,64]{1,0:T(1,128)}, f32[1,64]{1,0:T(1,128)S(1)}, u32[]{:S(2)}) copy-start(f32[1,64]{1,0:T(1,128)S(1)} %get-tuple-element.34) | copy-start | bytes 772
  21.5 3.8 %copy-start.1 = (f32[3,64,8,128]{3,2,1,0:T(8,128)S(1)}, f32[3,64,8,128]{3,2,1,0:T(8,128)}, u32[]{:S(2)}) copy-start(f32[3,64,8,128]{3,2,1,0:T(8,128)} %refs_0_.3) | copy-start | bytes 2359300
  22.2 1.3 %copy-start.4 = (bf16[512,2048]{1,0:T(8,128)(2,1)}, bf16[512,2048]{1,0:T(8,128)(2,1)S(1)}, u32[]{:S(2)}) copy-start(bf16[512,2048]{1,0:T(8,128)(2,1)S(1)} %tanh_convert_fusion) | copy-start | bytes 6291460
  23.5 11.0 %copy-start.7 = (f32[3,64,8,128]{3,2,1,0:T(8,128)S(1)}, f32[3,64,8,128]{3,2,1,0:T(8,128)}, u32[]{:S(2)}) copy-start(f32[3,64,8,128]{3,2,1,0:T(8,128)} %param.9) | copy-start | bytes 2359300
  34.5 2.0 %copy-start.2 = (f32[3,64,8,128]{3,2,1,0:T(8,128)}, f32[3,64,8,128]{3,2,1,0:T(8,128)S(1)}, u32[]{:S(2)}) copy-start(f32[3,64,8,128]{3,2,1,0:T(8,128)S(1)} %get-tuple-element.16.refs_3_) | copy-start | bytes 2359300
  36.6 1.5 %copy-start.9 = (f32[6,1024]{1,0:T(8,128)S(1)}, f32[6,1024]{1,0:T(8,128)}, u32[]{:S(2)}) copy-start(f32[6,1024]{1,0:T(8,128)} %reshape_reshape.3) | copy-start | bytes 73732
  36.6 1.5 %copy-start.13 = (f32[24]{0:T(128)S(1)}, f32[24]{0:T(128)}, u32[]{:S(2)}) copy-start(f32[24]{0:T(128)} %pad.16.clone) | copy-start | bytes 292
  36.9 1.2 %copy-start.6 = (f32[6,8,128,66]{2,1,3,0:T(8,128)}, f32[6,8,128,66]{2,1,3,0:T(8,128)S(1)}, u32[]{:S(2)}) copy-start(f32[6,8,128,66]{2,1,3,0:T(8,128)S(1)} %copy.53) | copy-start | bytes 4866052
  36.9 8.8 %copy-start.12 = (f32[4]{0:T(128)S(1)}, f32[4]{0:T(128)}, u32[]{:S(2)}) copy-start(f32[4]{0:T(128)} %get-tuple-element.32) | copy-start | bytes 52
  45.0 4.2 %copy-start.5 = (bf16[512,2048]{1,0:T(8,128)(2,1)S(1)}, bf16[512,2048]{1,0:T(8,128)(2,1)}, u32[]{:S(2)}) copy-start(bf16[512,2048]{1,0:T(8,128)(2,1)} %copy-done.4) | copy-start | bytes 6291460
  52.9 0.7 copy-start.14
  52.9 2.1 %copy-start.8 = (f32[512,128]{1,0:T(8,128)S(1)}, f32[512,128]{1,0:T(8,128)}, u32[]{:S(2)}) copy-start(f32[512,128]{1,0:T(8,128)} %fusion.6) | copy-start | bytes 786436
  57.1 19.6 %copy-start.3 = (f32[3,64,8,128]{3,2,1,0:T(8,128)S(1)}, f32[3,64,8,128]{3,2,1,0:T(8,128)}, u32[]{:S(2)}) copy-start(f32[3,64,8,128]{3,2,1,0:T(8,128)} %copy-done.2) | copy-start | bytes 2359300
